TPU v7x, 256 devices: a whole 4x4x8 slice. The times are simulated.
256 devices in a mesh: dp: 32 (over z_hi, y, core), tensor: 8 (over z_lo, x).
Axes of the slice: x: 4, y: 4, z: 8 (z_hi: 4, z_lo: 2; z = z_hi * 2 + z_lo), core: 2. Of those that a mesh axis runs over, the one named last changes fastest.
Arguments:
- activations: bfloat16 [4096, 8192], P('dp', 'tensor'), may hold values from -12 to 12
- hidden_grad: bfloat16 [4096, 14336], P('dp', 'tensor'), may hold values from -0.049804688 to 0.049804688
- master: float32 [8192, 14336], P('dp', 'tensor'), may hold values from -400 to 400
- moment_one: float32 [8192, 14336], P('dp', 'tensor'), may hold values from -100 to 100
- moment_two: float32 [8192, 14336], P('dp', 'tensor'), may hold values from 0.0001 to 0.01
Outputs:
- input_grad: bfloat16 [4096, 8192], P(('dp', 'tensor'))
- update: float32 [8192, 14336], P('dp', 'tensor')
- new_one: float32 [8192, 14336], P('dp', 'tensor')
- new_two: float32 [8192, 14336], P('dp', 'tensor')
All inputs are finite; a program needn't handle non-finite values.
Results may differ from a plain program's by a relative error of at most 0.0049.
Values may be sent and summed in bfloat16 or wider, within the bound.
No kernel may reach another device: no remote copies, remote signals or barrier semaphores. Data moves between devices by JAX's collectives and lax.ppermute only.
A program may use at most 128 MiB of HBM per device.

v0:
```python
import jax
import jax.numpy as jnp
from jax import lax
from jax.experimental import pallas as pl
from jax.experimental.pallas import tpu as pltpu
from jax.sharding import Mesh, PartitionSpec as P

beta_one = 0.9
beta_two = 0.999
corr_one = 1.0 - 0.9**10
corr_two = 1.0 - 0.999**10
adam_eps = 1e-06
decay = 0.01

DP = ("zh", "y", "c")
TP = ("zl", "x")
CH = ("zh", "y")
BF = jnp.bfloat16
F32 = jnp.float32


def shift(value, axis, by, size=4):
    return lax.ppermute(value, axis, [(i, (i - by) % size) for i in range(size)])


def ends(value, axis):
    return shift(value, axis, 1), shift(value, axis, 3)


def middle(one, three, axis):
    half = one.shape[0] // 2
    return shift(one[:half], axis, 1), shift(three[half:], axis, 3)


def rolled(value, axis, by):
    return lax.dynamic_slice_in_dim(jnp.concatenate([value, value], axis), by, 4, axis)


def dot(a, b, da, db):
    return lax.dot_general(a, b, (((da,), (db,)), ((), ())), preferred_element_type=F32)


def thirds(value):
    one = lax.reduce_precision(value, 8, 7)
    two = lax.reduce_precision(value - one, 8, 7)
    three = lax.reduce_precision(value - one - two, 8, 7)
    return jnp.concatenate([one, two, three]).astype(BF)


sync = lambda *values: lax.optimization_barrier(values)
cat = lambda *values: jnp.concatenate(values, 0)


def params(limit=56):
    return pltpu.CompilerParams(dimension_semantics=("arbitrary",), vmem_limit_bytes=limit << 20)


def fetch(pieces, tokens_ref, sems):
    copies, at = [], 0
    for i, piece in enumerate(pieces):
        size = piece.shape[0]
        copies.append(pltpu.make_async_copy(piece, tokens_ref.at[pl.ds(at, size)], sems.at[i]))
        copies[-1].start()
        at += size
    return copies


def part_kernel(*refs):
    pieces, (weight_ref, part_ref, tokens_ref, sems) = refs[:6], refs[6:]
    copies = fetch(pieces, tokens_ref, sems)
    for half in range(2):
        for copy in copies[1:] if half else copies[:1]:
            copy.wait()
        part = dot(tokens_ref[1024 * half : 1024 * half + 1024], weight_ref[...], 1, 1)
        part_ref[:, 16 * half : 16 * half + 16] = part.reshape(16, 8, 8, 512).swapaxes(0, 1).astype(BF)


def grad_kernel(*refs):
    pieces, (feats_ref, grad_ref, grad_other_ref, tokens_ref, sems) = refs[:6], refs[6:]
    for copy in fetch(pieces, tokens_ref, sems):
        copy.wait()
    grad = dot(feats_ref[...], tokens_ref[...], 1, 0)
    grad_ref[...] = grad[:256]
    grad_other_ref[...] = grad[256:]


def place_kernel(places_ref, got_ref, out_ref):
    for i in range(16):
        out_ref[places_ref[i], :8] = jnp.sum(got_ref[:, 16 + i].astype(F32), 0)
        out_ref[i, 8:] = jnp.sum(got_ref[:, i].astype(F32), 0)


def last_kernel(
    grad_ref, other_ref, one_ref, two_ref, master_ref, new_one_ref, new_two_ref, direction_ref, sums_ref, acc_ref
):
    step = pl.program_id(0)

    @pl.when(step == 0)
    def _():
        acc_ref[...] = jnp.zeros_like(acc_ref)

    grad = grad_ref[...] + other_ref[...]
    master = master_ref[...]
    new_one = beta_one * one_ref[...] + (1.0 - beta_one) * grad
    new_two = beta_two * two_ref[...] + (1.0 - beta_two) * grad * grad
    direction = new_one / corr_one / (jnp.sqrt(new_two / corr_two) + adam_eps) + decay * master
    new_one_ref[...] = new_one
    new_two_ref[...] = new_two
    direction_ref[...] = direction
    fold = lambda value: jnp.sum((value * value).reshape(-1, 8, 1792), 0)
    acc_ref[0] += fold(master)
    acc_ref[1] += fold(direction)

    @pl.when(step == pl.num_programs(0) - 1)
    def _():
        lane = lax.broadcasted_iota(jnp.int32, sums_ref.shape, 1)
        sums_ref[...] = jnp.where(
            lane == 0, jnp.sum(acc_ref[0]), jnp.where(lane == 1, jnp.sum(acc_ref[1]), 0.0)
        )


def whole(*shape):
    return pl.BlockSpec(shape, lambda i: (0,) * len(shape))


def cost(flops, size):
    return pl.CostEstimate(flops=flops, bytes_accessed=size, transcendentals=0)


def on_device(activations, hidden_grad, master, moment_one, moment_two):
    zh, y, c = (lax.axis_index(n) for n in DP)
    f32 = jax.ShapeDtypeStruct((256, 1792), F32)

    halves = hidden_grad.reshape(8, 2, 8, 1792)
    second = lax.all_gather(halves[:, 1].reshape(64, 1792), CH, axis=0, tiled=True)
    mine = halves[:, 0].reshape(64, 1792)

    z1, z3 = ends(mine, "zh")
    rows = lax.all_to_all(activations, TP, split_axis=0, concat_axis=1, tiled=True)
    z1, z3, rows, master_late = sync(z1, z3, rows, master)
    z2 = middle(z1, z3, "zh")
    rows = lax.all_to_all(rows, CH, split_axis=1, concat_axis=0, tiled=True)
    *z2, rows = sync(*z2, rows)

    y0 = cat(mine, z1, *z2, z3)
    y1, y3 = ends(y0, "y")
    rows = lax.dynamic_slice_in_dim(jnp.concatenate([rows, rows[:, :256]], 1), 256 * c, 512, 1)
    rows = rows.reshape(4, 4, 2, 8, 512).transpose(2, 1, 0, 3, 4)
    rows = jnp.stack([rows[1].swapaxes(0, 1), rolled(rolled(rows[0], 0, y), 1, zh)])
    copies = jnp.broadcast_to(rows.reshape(1, 2, 16, 8, 512), (8, 2, 16, 8, 512))
    feats = lax.all_to_all(copies, TP, split_axis=0, concat_axis=0, tiled=True)
    y1, y3, _ = sync(y1, y3, copies)
    *y2, second = sync(*middle(y1, y3, "y"), second)

    weight = master_late.astype(BF)
    weight_other = shift(weight, "c", 1, 2)
    both = jnp.where(c == 0, cat(weight, weight_other), cat(weight_other, weight))
    both, second = sync(both, second)

    feats = feats.transpose(4, 1, 2, 0, 3).reshape(512, 2048)
    *y2, both, feats, y0, y1, y3, second = sync(*y2, both, feats, y0, y1, y3, second)

    vmem, anywhere = (pl.BlockSpec(memory_space=space) for space in (pltpu.VMEM, pl.ANY))
    pieces = (second, y0, y1, *y2, y3)
    scratch = [pltpu.VMEM((2048, 1792), BF), pltpu.SemaphoreType.DMA((6,))]
    limit = pltpu.CompilerParams(vmem_limit_bytes=48 << 20)
    part = pl.pallas_call(
        part_kernel,
        in_specs=[anywhere] * 6 + [vmem],
        out_specs=vmem,
        out_shape=jax.ShapeDtypeStruct((8, 32, 8, 512), BF),
        scratch_shapes=scratch,
        compiler_params=limit,
        cost_estimate=cost(2 * 2048 * 512 * 1792, 12 << 20),
    )(*pieces, both)
    got = lax.all_to_all(part, TP, split_axis=0, concat_axis=0, tiled=True)
    feats, _ = sync(feats, part)
    grad, grad_other = pl.pallas_call(
        grad_kernel,
        in_specs=[anywhere] * 6 + [vmem],
        out_specs=[vmem] * 2,
        out_shape=[f32] * 2,
        scratch_shapes=scratch,
        compiler_params=limit,
        cost_estimate=cost(2 * 2048 * 512 * 1792, 12 << 20),
    )(*pieces, feats)
    grad_other = shift(grad_other, "c", 1, 2)
    places = jnp.stack([4 * ((zh + z) % 4) + (y + k) % 4 for k in range(4) for z in range(4)])
    out = pl.pallas_call(
        place_kernel,
        out_shape=jax.ShapeDtypeStruct((16, 16, 512), F32),
        in_specs=[pl.BlockSpec(memory_space=pltpu.SMEM)] + [pl.BlockSpec(memory_space=pltpu.VMEM)],
        compiler_params=pltpu.CompilerParams(vmem_limit_bytes=8 << 20),
        cost_estimate=cost(0, 2 << 20),
    )(places.astype(jnp.int32), got)
    slab = pl.BlockSpec((64, 1792), lambda i: (i, 0))
    new_one, new_two, direction, sums = pl.pallas_call(
        last_kernel,
        grid=(4,),
        in_specs=[slab] * 5,
        out_specs=[slab] * 3 + [whole(16, 128)],
        out_shape=[f32] * 3 + [jax.ShapeDtypeStruct((16, 128), F32)],
        scratch_shapes=[pltpu.VMEM((2, 8, 1792), F32)],
        compiler_params=params(),
        cost_estimate=cost(0, 8 << 20),
    )(grad, grad_other, moment_one, moment_two, master)
    sums, out = sync(sums, out)
    sums = jnp.sum(lax.all_to_all(sums, ("c",) + TP, split_axis=0, concat_axis=0, tiled=True), 0)[:2]

    extra = jnp.broadcast_to(jnp.pad(thirds(sums), (0, 506)), (16, 8, 512))
    out = jnp.concatenate([out.astype(BF), extra], 1)
    out = lax.all_to_all(out, CH, split_axis=0, concat_axis=0, tiled=True)
    input_grad = out[:, :16].transpose(1, 0, 2).reshape(16, 8192)
    sums = jnp.sum(out[:, 16, :6].astype(F32).reshape(16, 3, 2), (0, 1))
    trust = jnp.sqrt(sums[0]) / (jnp.sqrt(sums[1]) + adam_eps)
    return (input_grad, trust * direction, new_one, new_two)


def solution(mesh):
    fine = Mesh(mesh.devices.reshape(4, 4, 2, 2, 4), DP + TP)
    return jax.shard_map(
        on_device,
        mesh=fine,
        in_specs=(P(DP, TP),) * 5,
        out_specs=(P(DP + TP, None), P(DP, TP), P(DP, TP), P(DP, TP)),
        check_vma=False,
    )
```

profile of v0, /device:TPU:1, one launch (start us, length us, event | category | flops | bytes accessed | tf_op | source)
XLA Modules:
  0.0 201.0 jit_solution(1785531416175879277)
XLA Ops:
  7.2 0.0 all-gather.2.cloned.1.call-start
  7.2 1.8 slice_bitcast_fusion.1
  9.0 0.0 all-gather.2.cloned.1.call-update
  9.0 6.2 %all-to-all-start = ((bf16[8,16,1024]{2,1,0:T(8,128)(2,1)}), bf16[8,16,1024]{2,1,0:T(8,128)(2,1)S(1)}, u32[]{:S(2)}, u32[]{:S(2)}) async-start(bf16[8,16,1024]{2,1,0:T(8,128)(2,1)} %bitcast.72), calls=%async_computation | async-start | bytes 524288 | tf_op jit(solution)/shard_map/all_to_all | solution.py:139
  15.2 3.0 %collective-permute-start.1 = (bf16[64,1792]{1,0:T(8,128)(2,1)S(1)}, bf16[64,1792]{1,0:T(8,128)(2,1)S(1)}, u32[]{:S(2)}, u32[]{:S(2)}) collective-permute-start(bf16[64,1792]{1,0:T(8,128)(2,1)S(1)} %get-tuple-element.67), channel_id=1, source_target_pairs={{0,64},{64,128},{128,192},{192,0},{1,65},{65,129},{129,193},{193,1... | collective-permute-start | bytes 688136 | tf_op jit(solution)/shard_map/ppermute | solution.py:23
  18.2 2.2 %collective-permute-start = (bf16[64,1792]{1,0:T(8,128)(2,1)S(1)}, bf16[64,1792]{1,0:T(8,128)(2,1)S(1)}, u32[]{:S(2)}, u32[]{:S(2)}) collective-permute-start(bf16[64,1792]{1,0:T(8,128)(2,1)S(1)} %get-tuple-element.67), channel_id=1, source_target_pairs={{0,192},{64,0},{128,64},{192,128},{1,193},{65,1},{129,65},{193,129... | collective-permute-start | bytes 688136 | tf_op jit(solution)/shard_map/ppermute | solution.py:23
  20.4 0.9 all-to-all-done
  21.4 12.8 %collective-permute-done.1 = bf16[64,1792]{1,0:T(8,128)(2,1)S(1)} collective-permute-done((bf16[64,1792]{1,0:T(8,128)(2,1)S(1)}, bf16[64,1792]{1,0:T(8,128)(2,1)S(1)}, u32[]{:S(2)}, u32[]{:S(2)}) %collective-permute-start.1) | collective-permute-done | bytes 229408 | tf_op jit(solution)/shard_map/ppermute | solution.py:23
  34.2 0.0 collective-permute-done
  34.2 0.7 copy.40
  34.9 5.1 %all-to-all-start.1 = ((bf16[16,16,512]{2,0,1:T(8,128)(2,1)}), bf16[16,16,512]{2,0,1:T(8,128)(2,1)S(1)}, u32[]{:S(2)}, u32[]{:S(2)}) async-start(bf16[16,16,512]{2,0,1:T(8,128)(2,1)} %bitcast.61), calls=%async_computation.1 | async-start | bytes 524288 | tf_op jit(solution)/shard_map/all_to_all | solution.py:142
  40.1 2.3 %collective-permute-start.3 = (bf16[32,1792]{1,0:T(8,128)(2,1)S(1)}, bf16[32,1792]{1,0:T(8,128)(2,1)S(1)}, u32[]{:S(2)}, u32[]{:S(2)}) collective-permute-start(bf16[32,1792]{1,0:T(8,128)(2,1)S(1)} %slice.44), channel_id=1, source_target_pairs={{0,64},{64,128},{128,192},{192,0},{1,65},{65,129},{129,193},{193,1... | collective-permute-start | bytes 344072 | tf_op jit(solution)/shard_map/ppermute | solution.py:23
  42.4 1.3 collective-permute-start.2
  43.8 4.1 %collective-permute-done.3 = bf16[32,1792]{1,0:T(8,128)(2,1)S(1)} collective-permute-done((bf16[32,1792]{1,0:T(8,128)(2,1)S(1)}, bf16[32,1792]{1,0:T(8,128)(2,1)S(1)}, u32[]{:S(2)}, u32[]{:S(2)}) %collective-permute-start.3) | collective-permute-done | bytes 114720 | tf_op jit(solution)/shard_map/ppermute | solution.py:23
  47.8 1.9 collective-permute-done.2
  49.8 0.5 all-to-all-done.1
  50.3 0.1 fusion
  50.4 0.1 fusion.2
  50.5 0.1 fusion.1
  50.6 1.6 broadcast_in_dim.11
  52.2 10.2 %all-to-all-start.2 = ((bf16[8,2,16,8,512]{4,3,2,1,0:T(8,128)(2,1)}), bf16[8,2,16,8,512]{4,3,2,1,0:T(8,128)(2,1)}, u32[]{:S(2)}, u32[]{:S(2)}) async-start(bf16[8,2,16,8,512]{4,3,2,1,0:T(8,128)(2,1)} %broadcast_in_dim.11), calls=%async_computation.2 | async-start | bytes 4194304 | tf_op jit(solution)/shard_map/all_to_all | solution.py:151
  62.5 0.0 copy-start.4
  62.5 1.0 collective-permute-start.5
  63.5 1.7 collective-permute-start.4
  65.3 1.0 convert_element_type.14
  66.3 3.3 %collective-permute-start.8 = (bf16[256,1792]{1,0:T(8,128)(2,1)}, bf16[256,1792]{1,0:T(8,128)(2,1)}, u32[]{:S(2)}, u32[]{:S(2)}) collective-permute-start(bf16[256,1792]{1,0:T(8,128)(2,1)} %convert_element_type.14), channel_id=1, source_target_pairs={{0,8},{8,0},{1,9},{9,1},{2,10},{10,2},{3,11},{11,3},{4,12},{12,4},... | collective-permute-start | bytes 2752520 | tf_op jit(solution)/shard_map/ppermute | solution.py:23
  69.6 23.8 %collective-permute-done.5.refs_5_ = bf16[256,1792]{1,0:T(8,128)(2,1)S(1)} collective-permute-done((bf16[256,1792]{1,0:T(8,128)(2,1)S(1)}, bf16[256,1792]{1,0:T(8,128)(2,1)S(1)}, u32[]{:S(2)}, u32[]{:S(2)}) %collective-permute-start.5) | collective-permute-done | bytes 917536 | tf_op jit(solution)/shard_map/ppermute | solution.py:23
  93.4 0.0 collective-permute-done.4.refs_2_
  93.4 0.8 slice.48
  94.2 0.9 copy-done.1
  95.1 0.8 slice.49
  95.9 0.0 collective-permute-start.7
  95.9 2.7 %collective-permute-start.6 = (bf16[128,1792]{1,0:T(8,128)(2,1)}, bf16[128,1792]{1,0:T(8,128)(2,1)}, u32[]{:S(2)}, u32[]{:S(2)}) collective-permute-start(bf16[128,1792]{1,0:T(8,128)(2,1)} %slice.48), channel_id=1, source_target_pairs={{0,48},{16,0},{32,16},{48,32},{1,49},{17,1},{33,17},{49,33},{2,50}... | collective-permute-start | bytes 1376264 | tf_op jit(solution)/shard_map/ppermute | solution.py:23
  98.6 0.0 collective-permute-done.8
  98.6 2.6 %maximum_select_fusion.refs_6_ = bf16[512,1792]{1,0:T(8,128)(2,1)S(1)} fusion(bf16[256,1792]{1,0:T(8,128)(2,1)} %collective-permute-done.8, bf16[256,1792]{1,0:T(8,128)(2,1)} %convert_element_type.14, pred[]{:T(512)S(6)} %eq.36), kind=kLoop, calls=%fused_computation | loop fusion | flops 8257536 | bytes 3670017 | tf_op jit(solution)/shard_map/jit(_where)/select_n | solution.py:157
  101.2 7.7 %all-to-all-done.2 = bf16[8,2,16,8,512]{4,3,2,1,0:T(8,128)(2,1)} async-done(((bf16[8,2,16,8,512]{4,3,2,1,0:T(8,128)(2,1)}), bf16[8,2,16,8,512]{4,3,2,1,0:T(8,128)(2,1)}, u32[]{:S(2)}, u32[]{:S(2)}) %all-to-all-start.2) | async-done | bytes 2097184 | tf_op jit(solution)/shard_map/all_to_all | solution.py:151
  108.9 3.2 %copy.30 = bf16[8,2,16,8,512]{4,3,0,2,1:T(8,128)(2,1)} copy(bf16[8,2,16,8,512]{4,3,2,1,0:T(8,128)(2,1)} %all-to-all-done.2) | data formatting | bytes 4194304 | tf_op jit(solution)/shard_map/all_to_all | solution.py:151
  112.1 0.0 collective-permute-done.7.refs_4_
  112.1 0.0 collective-permute-done.6.refs_3_
  112.1 0.0 all-gather.2.cloned.1.call-done.refs_0_
  112.2 0.0 copy-start.2
  112.2 1.2 copy-done.2
  113.3 1.2 copy-done.5
  114.5 7.6 %shard_map.84 = bf16[8,32,8,512]{3,2,1,0:T(8,128)(2,1)} custom-call(bf16[1024,1792]{1,0:T(8,128)(2,1)} %all-gather.2.cloned.1.call-done.refs_0_, bf16[256,1792]{1,0:T(8,128)(2,1)S(1)} %copy-done.5, bf16[256,1792]{1,0:T(8,128)(2,1)S(1)} %copy-done.2, bf16[128,1792]{1,0:T(8,128)(2,1)} %collective-permute-done.6.refs_3_, ...), custom_call_target="tpu_custom_call" | custom-call | flops 3758096384 | bytes 12582912 | tf_op jit(solution)/shard_map/pallas_call | solution.py:167
  122.1 4.2 %all-to-all-start.3 = ((bf16[8,32,8,512]{3,2,1,0:T(8,128)(2,1)}), bf16[8,32,8,512]{3,2,1,0:T(8,128)(2,1)S(1)}, u32[]{:S(2)}, u32[]{:S(2)}) async-start(bf16[8,32,8,512]{3,2,1,0:T(8,128)(2,1)} %shard_map.84), calls=%async_computation.3 | async-start | bytes 4194304 | tf_op jit(solution)/shard_map/all_to_all | solution.py:176
  126.3 3.9 %copy.31.refs_6_ = bf16[512,2048]{1,0:T(8,128)(2,1)} copy(bf16[512,2048]{0,1:T(8,128)(2,1)} %bitcast.62) | data formatting | bytes 4194304 | tf_op jit(solution)/shard_map/optimization_barrier | solution.py:50
  130.3 1.2 copy-done.3
  131.5 1.2 copy-done.6
  132.6 9.0 %shard_map.85 = (f32[256,1792]{1,0:T(8,128)S(1)}, f32[256,1792]{1,0:T(8,128)}) custom-call(bf16[1024,1792]{1,0:T(8,128)(2,1)} %all-gather.2.cloned.1.call-done.refs_0_, bf16[256,1792]{1,0:T(8,128)(2,1)S(1)} %copy-done.6, bf16[256,1792]{1,0:T(8,128)(2,1)S(1)} %copy-done.3, bf16[128,1792]{1,0:T(8,128)(2,1)} %collective-permute-done.6.refs_3_, ...), custom_call_target="tpu_custom_call" | custom-call | flops 3758096384 | bytes 12582912 | tf_op jit(solution)/shard_map/pallas_call | solution.py:178
  141.7 1.3 copy-done
  143.0 1.3 collective-permute-start.9
  144.3 0.1 stack.79.places_ref
  144.4 3.7 %collective-permute-done.9.other_ref = f32[256,1792]{1,0:T(8,128)} collective-permute-done((f32[256,1792]{1,0:T(8,128)}, f32[256,1792]{1,0:T(8,128)}, u32[]{:S(2)}, u32[]{:S(2)}) %collective-permute-start.9) | collective-permute-done | bytes 1835040 | tf_op jit(solution)/shard_map/ppermute | solution.py:23
  148.0 7.2 %shard_map.86 = (f32[256,1792]{1,0:T(8,128)}, f32[256,1792]{1,0:T(8,128)}, f32[256,1792]{1,0:T(8,128)}, f32[16,128]{1,0:T(8,128)}) custom-call(f32[256,1792]{1,0:T(8,128)} %copy-done, f32[256,1792]{1,0:T(8,128)} %collective-permute-done.9.other_ref, f32[256,1792]{1,0:T(8,128)} %one_ref.1, f32[256,1792]{1,0:T(8,128)} %two_ref.1, f32[256,1792]{1,0:T(8,128)} %master_ref.1), custom_call_target="tpu_custom_call" | custom-call | bytes 8388608 | tf_op jit(solution)/shard_map/pallas_call | solution.py:197
  155.2 0.8 shard_map.87
  156.0 0.0 copy-start.8
  156.1 6.2 %all-to-all-start.4 = ((f32[16,1,128]{2,1,0:T(1,128)}), f32[16,1,128]{2,1,0:T(1,128)S(1)}, u32[]{:S(2)}, u32[]{:S(2)}) async-start(f32[16,1,128]{2,1,0:T(1,128)} %bitcast.35), calls=%async_computation.4 | async-start | bytes 16384 | tf_op jit(solution)/shard_map/all_to_all | solution.py:208
  162.3 5.4 %all-to-all-done.4 = f32[16,1,128]{2,1,0:T(1,128)S(1)} async-done(((f32[16,1,128]{2,1,0:T(1,128)}), f32[16,1,128]{2,1,0:T(1,128)S(1)}, u32[]{:S(2)}, u32[]{:S(2)}) %all-to-all-start.4) | async-done | bytes 8224 | tf_op jit(solution)/shard_map/all_to_all | solution.py:208
  167.8 0.1 fusion.8
  167.9 22.0 %all_to_all.62 = bf16[16,24,512]{2,1,0:T(8,128)(2,1)S(1)} all-to-all(bf16[16,24,512]{2,1,0:T(8,128)(2,1)S(1)} %pad_maximum_fusion), channel_id=1, replica_groups=mesh['zh'=4,'y'=4,'c'=2,'zl'=2,'x'=4] {'zh','y'}, dimensions={0} | all-to-all | bytes 786432 | tf_op jit(solution)/shard_map/all_to_all | solution.py:212
  189.9 0.7 copy.38
  190.7 0.1 reduce_sum.27
  190.8 0.6 fusion.12
  192.8 1.4 broadcast_multiply_fusion
  (32 shorter events, 0.4 us)
Async XLA Ops:
  7.2 105.0 %all-gather.2.cloned.1.call-start = ((), (), s32[]{:S(2)}) async-start(), calls=%async_computation.6 | async-start | bytes 3899392 | tf_op jit(solution)/shard_map/all_gather | solution.py:135
  9.0 12.3 %all-to-all-start = ((bf16[8,16,1024]{2,1,0:T(8,128)(2,1)}), bf16[8,16,1024]{2,1,0:T(8,128)(2,1)S(1)}, u32[]{:S(2)}, u32[]{:S(2)}) async-start(bf16[8,16,1024]{2,1,0:T(8,128)(2,1)} %bitcast.72), calls=%async_computation | async-start | bytes 524288 | tf_op jit(solution)/shard_map/all_to_all | solution.py:139
  15.2 19.0 %collective-permute-start.1 = (bf16[64,1792]{1,0:T(8,128)(2,1)S(1)}, bf16[64,1792]{1,0:T(8,128)(2,1)S(1)}, u32[]{:S(2)}, u32[]{:S(2)}) collective-permute-start(bf16[64,1792]{1,0:T(8,128)(2,1)S(1)} %get-tuple-element.67), channel_id=1, source_target_pairs={{0,64},{64,128},{128,192},{192,0},{1,65},{65,129},{129,193},{193,1... | collective-permute-start | bytes 688136 | tf_op jit(solution)/shard_map/ppermute | solution.py:23
  18.2 16.0 %collective-permute-start = (bf16[64,1792]{1,0:T(8,128)(2,1)S(1)}, bf16[64,1792]{1,0:T(8,128)(2,1)S(1)}, u32[]{:S(2)}, u32[]{:S(2)}) collective-permute-start(bf16[64,1792]{1,0:T(8,128)(2,1)S(1)} %get-tuple-element.67), channel_id=1, source_target_pairs={{0,192},{64,0},{128,64},{192,128},{1,193},{65,1},{129,65},{193,129... | collective-permute-start | bytes 688136 | tf_op jit(solution)/shard_map/ppermute | solution.py:23
  34.9 15.4 %all-to-all-start.1 = ((bf16[16,16,512]{2,0,1:T(8,128)(2,1)}), bf16[16,16,512]{2,0,1:T(8,128)(2,1)S(1)}, u32[]{:S(2)}, u32[]{:S(2)}) async-start(bf16[16,16,512]{2,0,1:T(8,128)(2,1)} %bitcast.61), calls=%async_computation.1 | async-start | bytes 524288 | tf_op jit(solution)/shard_map/all_to_all | solution.py:142
  40.1 7.7 %collective-permute-start.3 = (bf16[32,1792]{1,0:T(8,128)(2,1)S(1)}, bf16[32,1792]{1,0:T(8,128)(2,1)S(1)}, u32[]{:S(2)}, u32[]{:S(2)}) collective-permute-start(bf16[32,1792]{1,0:T(8,128)(2,1)S(1)} %slice.44), channel_id=1, source_target_pairs={{0,64},{64,128},{128,192},{192,0},{1,65},{65,129},{129,193},{193,1... | collective-permute-start | bytes 344072 | tf_op jit(solution)/shard_map/ppermute | solution.py:23
  42.4 7.3 %collective-permute-start.2 = (bf16[32,1792]{1,0:T(8,128)(2,1)S(1)}, bf16[32,1792]{1,0:T(8,128)(2,1)S(1)}, u32[]{:S(2)}, u32[]{:S(2)}) collective-permute-start(bf16[32,1792]{1,0:T(8,128)(2,1)S(1)} %slice.43), channel_id=1, source_target_pairs={{0,192},{64,0},{128,64},{192,128},{1,193},{65,1},{129,65},{193,129... | collective-permute-start | bytes 344072 | tf_op jit(solution)/shard_map/ppermute | solution.py:23
  52.2 10.2 %copy-start.9 = (bf16[128,1792]{1,0:T(8,128)(2,1)S(1)}, bf16[128,1792]{1,0:T(8,128)(2,1)}, u32[]{:S(2)}) copy-start(bf16[128,1792]{1,0:T(8,128)(2,1)} %param.6) | copy-start | bytes 1376260
  52.2 13.1 %copy-start.7 = (f32[256,1792]{1,0:T(8,128)S(1)}, f32[256,1792]{1,0:T(8,128)}, u32[]{:S(2)}) copy-start(f32[256,1792]{1,0:T(8,128)} %master_ref.1) | copy-start | bytes 5505028
  52.2 56.7 %all-to-all-start.2 = ((bf16[8,2,16,8,512]{4,3,2,1,0:T(8,128)(2,1)}), bf16[8,2,16,8,512]{4,3,2,1,0:T(8,128)(2,1)}, u32[]{:S(2)}, u32[]{:S(2)}) async-start(bf16[8,2,16,8,512]{4,3,2,1,0:T(8,128)(2,1)} %broadcast_in_dim.11), calls=%async_computation.2 | async-start | bytes 4194304 | tf_op jit(solution)/shard_map/all_to_all | solution.py:151
  62.5 31.7 %copy-start.4 = (bf16[256,1792]{1,0:T(8,128)(2,1)}, bf16[256,1792]{1,0:T(8,128)(2,1)S(1)}, u32[]{:S(2)}) copy-start(bf16[256,1792]{1,0:T(8,128)(2,1)S(1)} %constant_dynamic-update-slice_fusion.refs_1_) | copy-start | bytes 2752516
  62.5 30.8 %collective-permute-start.5 = (bf16[256,1792]{1,0:T(8,128)(2,1)S(1)}, bf16[256,1792]{1,0:T(8,128)(2,1)S(1)}, u32[]{:S(2)}, u32[]{:S(2)}) collective-permute-start(bf16[256,1792]{1,0:T(8,128)(2,1)S(1)} %constant_dynamic-update-slice_fusion.refs_1_), channel_id=1, source_target_pairs={{0,16},{16,32},{32,48},{48,0},{1,17},{17,33},{33,49},{49,1},{2,18}... | collective-permute-start | bytes 2752520 | tf_op jit(solution)/shard_map/ppermute | solution.py:23
  63.5 29.8 %collective-permute-start.4 = (bf16[256,1792]{1,0:T(8,128)(2,1)S(1)}, bf16[256,1792]{1,0:T(8,128)(2,1)S(1)}, u32[]{:S(2)}, u32[]{:S(2)}) collective-permute-start(bf16[256,1792]{1,0:T(8,128)(2,1)S(1)} %constant_dynamic-update-slice_fusion.refs_1_), channel_id=1, source_target_pairs={{0,48},{16,0},{32,16},{48,32},{1,49},{17,1},{33,17},{49,33},{2,50}... | collective-permute-start | bytes 2752520 | tf_op jit(solution)/shard_map/ppermute | solution.py:23
  66.3 32.3 %collective-permute-start.8 = (bf16[256,1792]{1,0:T(8,128)(2,1)}, bf16[256,1792]{1,0:T(8,128)(2,1)}, u32[]{:S(2)}, u32[]{:S(2)}) collective-permute-start(bf16[256,1792]{1,0:T(8,128)(2,1)} %convert_element_type.14), channel_id=1, source_target_pairs={{0,8},{8,0},{1,9},{9,1},{2,10},{10,2},{3,11},{11,3},{4,12},{12,4},... | collective-permute-start | bytes 2752520 | tf_op jit(solution)/shard_map/ppermute | solution.py:23
  94.2 0.9 copy-start.1
  95.9 16.2 %collective-permute-start.7 = (bf16[128,1792]{1,0:T(8,128)(2,1)}, bf16[128,1792]{1,0:T(8,128)(2,1)S(1)}, u32[]{:S(2)}, u32[]{:S(2)}) collective-permute-start(bf16[128,1792]{1,0:T(8,128)(2,1)} %slice.49), channel_id=1, source_target_pairs={{0,16},{16,32},{32,48},{48,0},{1,17},{17,33},{33,49},{49,1},{2,18}... | collective-permute-start | bytes 1376264 | tf_op jit(solution)/shard_map/ppermute | solution.py:23
  95.9 16.2 %collective-permute-start.6 = (bf16[128,1792]{1,0:T(8,128)(2,1)}, bf16[128,1792]{1,0:T(8,128)(2,1)}, u32[]{:S(2)}, u32[]{:S(2)}) collective-permute-start(bf16[128,1792]{1,0:T(8,128)(2,1)} %slice.48), channel_id=1, source_target_pairs={{0,48},{16,0},{32,16},{48,32},{1,49},{17,1},{33,17},{49,33},{2,50}... | collective-permute-start | bytes 1376264 | tf_op jit(solution)/shard_map/ppermute | solution.py:23
  112.2 1.2 copy-start.2
  113.3 1.2 copy-start.5
  122.1 33.1 %all-to-all-start.3 = ((bf16[8,32,8,512]{3,2,1,0:T(8,128)(2,1)}), bf16[8,32,8,512]{3,2,1,0:T(8,128)(2,1)S(1)}, u32[]{:S(2)}, u32[]{:S(2)}) async-start(bf16[8,32,8,512]{3,2,1,0:T(8,128)(2,1)} %shard_map.84), calls=%async_computation.3 | async-start | bytes 4194304 | tf_op jit(solution)/shard_map/all_to_all | solution.py:176
  130.3 1.2 copy-start.3
  131.5 1.2 copy-start.6
  141.7 1.3 copy-start
  143.0 5.1 %collective-permute-start.9 = (f32[256,1792]{1,0:T(8,128)}, f32[256,1792]{1,0:T(8,128)}, u32[]{:S(2)}, u32[]{:S(2)}) collective-permute-start(f32[256,1792]{1,0:T(8,128)} %get-tuple-element.59), channel_id=1, source_target_pairs={{0,8},{8,0},{1,9},{9,1},{2,10},{10,2},{3,11},{11,3},{4,12},{12,4},... | collective-permute-start | bytes 5505032 | tf_op jit(solution)/shard_map/ppermute | solution.py:23
  156.0 36.8 %copy-start.8 = (f32[256,1792]{1,0:T(8,128)S(1)}, f32[256,1792]{1,0:T(8,128)}, u32[]{:S(2)}) copy-start(f32[256,1792]{1,0:T(8,128)} %get-tuple-element.63) | copy-start | bytes 5505028
  156.1 11.6 %all-to-all-start.4 = ((f32[16,1,128]{2,1,0:T(1,128)}), f32[16,1,128]{2,1,0:T(1,128)S(1)}, u32[]{:S(2)}, u32[]{:S(2)}) async-start(f32[16,1,128]{2,1,0:T(1,128)} %bitcast.35), calls=%async_computation.4 | async-start | bytes 16384 | tf_op jit(solution)/shard_map/all_to_all | solution.py:208
Sparse Core Ops, SparseCore 0:
  10.4 88.5 all-gather.1
where the time goes:
time: 202 us; the launch traced here: 201 us
  waiting for transfers between devices  60.9 us (30%)
  starting transfers between devices  50.9 us (25%)
  Pallas kernels  24.6 us (12%)
  blocking collectives  22 us (11%)
  local copies, waits for them, and re-layouts  21.5 us (11%)
  between operations  15.7 us (8%)
  other arithmetic  5.44 us (3%)
    ppermute x10, waiting for transfers between devices, shift(): lax.ppermute(value, axis, [(i, (i - by) % size) for i in range(size)])  46.3 us
    all_to_all x1, blocking collectives, on_device(): out = lax.all_to_all(out, CH, split_axis=0, concat_axis=0, tiled=True)  22 us
    ppermute x10, starting transfers between devices, shift(): lax.ppermute(value, axis, [(i, (i - by) % size) for i in range(size)])  18.9 us
    all_to_all x1, starting transfers between devices, on_device(): feats = lax.all_to_all(copies, TP, split_axis=0, concat_axis=0, tiled=True)  10.2 us
    pallas_call x1, Pallas kernels, on_device(): pl.pallas_call(grad_kernel, in_specs=[anywhere] * 6 + [vmem], out_specs=[...  9.05 us
    all_to_all x1, waiting for transfers between devices, on_device(): feats = lax.all_to_all(copies, TP, split_axis=0, concat_axis=0, tiled=True)  7.74 us
    pallas_call x1, Pallas kernels, on_device(): pl.pallas_call(part_kernel, in_specs=[anywhere] * 6 + [vmem], out_specs=v...  7.6 us
    pallas_call x1, Pallas kernels, on_device(): pl.pallas_call(last_kernel, grid=(4,), in_specs=[slab] * 5, out_specs=[sl...  7.19 us
  transfers between devices with their start and end apart: 16, of which 9 were waited for; matrix products, arithmetic and copies ran while one was open for 8% of the time, Pallas kernels for 8%

commit v1 on v0

--- a/solution.py
+++ b/solution.py
@@ -51,7 +51,7 @@
 cat = lambda *values: jnp.concatenate(values, 0)
 
 
-def params(limit=56):
+def params(limit=60):
     return pltpu.CompilerParams(dimension_semantics=("arbitrary",), vmem_limit_bytes=limit << 20)
 
 
@@ -77,9 +77,11 @@
 
 def grad_kernel(*refs):
     pieces, (feats_ref, grad_ref, grad_other_ref, tokens_ref, sems) = refs[:6], refs[6:]
-    for copy in fetch(pieces, tokens_ref, sems):
+    copies = fetch(pieces, tokens_ref, sems)
+    feats = [feats_ref[:, i].astype(F32).swapaxes(0, 1).reshape(1024, 512).astype(BF) for i in range(2)]
+    for copy in copies:
         copy.wait()
-    grad = dot(feats_ref[...], tokens_ref[...], 1, 0)
+    grad = dot(jnp.concatenate(feats, 0), tokens_ref[...], 0, 0)
     grad_ref[...] = grad[:256]
     grad_other_ref[...] = grad[256:]
 
@@ -149,7 +151,6 @@
     rows = jnp.stack([rows[1].swapaxes(0, 1), rolled(rolled(rows[0], 0, y), 1, zh)])
     copies = jnp.broadcast_to(rows.reshape(1, 2, 16, 8, 512), (8, 2, 16, 8, 512))
     feats = lax.all_to_all(copies, TP, split_axis=0, concat_axis=0, tiled=True)
-    y1, y3, _ = sync(y1, y3, copies)
     *y2, second = sync(*middle(y1, y3, "y"), second)
 
     weight = master_late.astype(BF)
@@ -157,13 +158,12 @@
     both = jnp.where(c == 0, cat(weight, weight_other), cat(weight_other, weight))
     both, second = sync(both, second)
 
-    feats = feats.transpose(4, 1, 2, 0, 3).reshape(512, 2048)
-    *y2, both, feats, y0, y1, y3, second = sync(*y2, both, feats, y0, y1, y3, second)
-
-    vmem, anywhere = (pl.BlockSpec(memory_space=space) for space in (pltpu.VMEM, pl.ANY))
+    *y2, both, y0, y1, y3, second = sync(*y2, both, y0, y1, y3, second)
+
+    vmem, anywhere = (pl.BlockSpec(memory_space=space) for space in (pltpu.VMEM, pltpu.HBM))
     pieces = (second, y0, y1, *y2, y3)
     scratch = [pltpu.VMEM((2048, 1792), BF), pltpu.SemaphoreType.DMA((6,))]
-    limit = pltpu.CompilerParams(vmem_limit_bytes=48 << 20)
+    limit = pltpu.CompilerParams(vmem_limit_bytes=60 << 20)
     part = pl.pallas_call(
         part_kernel,
         in_specs=[anywhere] * 6 + [vmem],
@@ -193,10 +193,10 @@
         compiler_params=pltpu.CompilerParams(vmem_limit_bytes=8 << 20),
         cost_estimate=cost(0, 2 << 20),
     )(places.astype(jnp.int32), got)
-    slab = pl.BlockSpec((64, 1792), lambda i: (i, 0))
+    slab = pl.BlockSpec((128, 1792), lambda i: (i, 0))
     new_one, new_two, direction, sums = pl.pallas_call(
         last_kernel,
-        grid=(4,),
+        grid=(2,),
         in_specs=[slab] * 5,
         out_specs=[slab] * 3 + [whole(16, 128)],
         out_shape=[f32] * 3 + [jax.ShapeDtypeStruct((16, 128), F32)],

time: 202 us -> 192 us (0.950)
  local copies, waits for them, and re-layouts: 21.5 us -> 7.51 us
  starting transfers between devices: 50.9 us -> 54.7 us
  Pallas kernels: 24.6 us -> 26.8 us
  waiting for transfers between devices: 60.9 us -> 58.7 us
    all_to_all x1, waiting for transfers between devices: 7.74 us -> 0.01 us  [on_device(): feats = lax.all_to_all(copies, TP, split_axis=0, concat_axis=0, tiled=True)]
    unnamed x25 -> x19, local copies, waits for them, and re-layouts: 6.98 us -> 1.76 us
    optimization_barrier x1 -> x0, local copies, waits for them, and re-layouts: 3.95 us -> none  [sync = lambda *values: lax.optimization_barrier(values)]
    ppermute x10, waiting for transfers between devices: 46.3 us -> 49.8 us  [shift(): lax.ppermute(value, axis, [(i, (i - by) % size) for i in range(size)])]
    all_to_all x1 -> x0, local copies, waits for them, and re-layouts: 3.22 us -> none  [on_device(): feats = lax.all_to_all(copies, TP, split_axis=0, concat_axis=0, tiled=True)]
    ppermute x10, starting transfers between devices: 18.9 us -> 22 us  [shift(): lax.ppermute(value, axis, [(i, (i - by) % size) for i in range(size)])]
  transfers between devices with their start and end apart: 16 -> 16, of which waited for: 9 -> 10; matrix products, arithmetic and copies ran while one was open for 8% -> 3% of each run, Pallas kernels for 8% -> 14%
where the time goes in v1:
time: 192 us; the launch traced here: 191 us
  waiting for transfers between devices  58.7 us (31%)
  starting transfers between devices  54.7 us (28%)
  Pallas kernels  26.8 us (14%)
  blocking collectives  23.6 us (12%)
  between operations  15.7 us (8%)
  local copies, waits for them, and re-layouts  7.51 us (4%)
  other arithmetic  3.9 us (2%)
    ppermute x10, waiting for transfers between devices, shift(): lax.ppermute(value, axis, [(i, (i - by) % size) for i in range(size)])  49.8 us
    all_to_all x1, blocking collectives, on_device(): out = lax.all_to_all(out, CH, split_axis=0, concat_axis=0, tiled=True)  23.6 us
    ppermute x10, starting transfers between devices, shift(): lax.ppermute(value, axis, [(i, (i - by) % size) for i in range(size)])  22 us
    pallas_call x1, Pallas kernels, on_device(): pl.pallas_call(grad_kernel, in_specs=[anywhere] * 6 + [vmem], out_specs=[...  10.5 us
    all_to_all x1, starting transfers between devices, on_device(): feats = lax.all_to_all(copies, TP, split_axis=0, concat_axis=0, tiled=True)  10.5 us
    pallas_call x1, Pallas kernels, on_device(): pl.pallas_call(part_kernel, in_specs=[anywhere] * 6 + [vmem], out_specs=v...  9.11 us
    pallas_call x1, Pallas kernels, on_device(): pl.pallas_call(last_kernel, grid=(2,), in_specs=[slab] * 5, out_specs=[sl...  6.35 us
    all_to_all x1, starting transfers between devices, on_device(): lax.all_to_all(activations, TP, split_axis=0, concat_axis=1, tiled=True)  6.22 us
  transfers between devices with their start and end apart: 16, of which 10 were waited for; matrix products, arithmetic and copies ran while one was open for 3% of the time, Pallas kernels for 14%

profile of v1, /device:TPU:1, one launch (start us, length us, event | category | flops | bytes accessed | tf_op | source)
XLA Modules:
  0.0 190.9 jit_solution(11240415291486119360)
XLA Ops:
  7.2 0.0 all-gather.2.cloned.1.call-start
  7.2 1.8 slice_bitcast_fusion.1
  9.0 0.0 all-gather.2.cloned.1.call-update
  9.0 6.2 %all-to-all-start = ((bf16[8,16,1024]{2,1,0:T(8,128)(2,1)}), bf16[8,16,1024]{2,1,0:T(8,128)(2,1)S(1)}, u32[]{:S(2)}, u32[]{:S(2)}) async-start(bf16[8,16,1024]{2,1,0:T(8,128)(2,1)} %bitcast.68), calls=%async_computation | async-start | bytes 524288 | tf_op jit(solution)/shard_map/all_to_all | solution.py:141
  15.2 3.0 %collective-permute-start.1 = (bf16[64,1792]{1,0:T(8,128)(2,1)S(1)}, bf16[64,1792]{1,0:T(8,128)(2,1)S(1)}, u32[]{:S(2)}, u32[]{:S(2)}) collective-permute-start(bf16[64,1792]{1,0:T(8,128)(2,1)S(1)} %get-tuple-element.61), channel_id=1, source_target_pairs={{0,64},{64,128},{128,192},{192,0},{1,65},{65,129},{129,193},{193,1... | collective-permute-start | bytes 688136 | tf_op jit(solution)/shard_map/ppermute | solution.py:23
  18.2 2.2 %collective-permute-start = (bf16[64,1792]{1,0:T(8,128)(2,1)S(1)}, bf16[64,1792]{1,0:T(8,128)(2,1)S(1)}, u32[]{:S(2)}, u32[]{:S(2)}) collective-permute-start(bf16[64,1792]{1,0:T(8,128)(2,1)S(1)} %get-tuple-element.61), channel_id=1, source_target_pairs={{0,192},{64,0},{128,64},{192,128},{1,193},{65,1},{129,65},{193,129... | collective-permute-start | bytes 688136 | tf_op jit(solution)/shard_map/ppermute | solution.py:23
  20.4 0.9 all-to-all-done
  21.3 12.0 %collective-permute-done.1 = bf16[64,1792]{1,0:T(8,128)(2,1)S(1)} collective-permute-done((bf16[64,1792]{1,0:T(8,128)(2,1)S(1)}, bf16[64,1792]{1,0:T(8,128)(2,1)S(1)}, u32[]{:S(2)}, u32[]{:S(2)}) %collective-permute-start.1) | collective-permute-done | bytes 229408 | tf_op jit(solution)/shard_map/ppermute | solution.py:23
  33.3 0.0 collective-permute-done
  33.3 0.7 copy.36
  34.1 5.3 %all-to-all-start.1 = ((bf16[16,16,512]{2,0,1:T(8,128)(2,1)}), bf16[16,16,512]{2,0,1:T(8,128)(2,1)S(1)}, u32[]{:S(2)}, u32[]{:S(2)}) async-start(bf16[16,16,512]{2,0,1:T(8,128)(2,1)} %bitcast.58), calls=%async_computation.1 | async-start | bytes 524288 | tf_op jit(solution)/shard_map/all_to_all | solution.py:144
  39.4 2.3 %collective-permute-start.3 = (bf16[32,1792]{1,0:T(8,128)(2,1)S(1)}, bf16[32,1792]{1,0:T(8,128)(2,1)S(1)}, u32[]{:S(2)}, u32[]{:S(2)}) collective-permute-start(bf16[32,1792]{1,0:T(8,128)(2,1)S(1)} %slice.44), channel_id=1, source_target_pairs={{0,64},{64,128},{128,192},{192,0},{1,65},{65,129},{129,193},{193,1... | collective-permute-start | bytes 344072 | tf_op jit(solution)/shard_map/ppermute | solution.py:23
  41.7 1.3 collective-permute-start.2
  43.1 4.4 %collective-permute-done.3 = bf16[32,1792]{1,0:T(8,128)(2,1)S(1)} collective-permute-done((bf16[32,1792]{1,0:T(8,128)(2,1)S(1)}, bf16[32,1792]{1,0:T(8,128)(2,1)S(1)}, u32[]{:S(2)}, u32[]{:S(2)}) %collective-permute-start.3) | collective-permute-done | bytes 114720 | tf_op jit(solution)/shard_map/ppermute | solution.py:23
  47.5 0.0 collective-permute-done.2
  47.5 2.3 %all-to-all-done.1 = bf16[16,16,512]{2,0,1:T(8,128)(2,1)S(1)} async-done(((bf16[16,16,512]{2,0,1:T(8,128)(2,1)}), bf16[16,16,512]{2,0,1:T(8,128)(2,1)S(1)}, u32[]{:S(2)}, u32[]{:S(2)}) %all-to-all-start.1) | async-done | bytes 262176 | tf_op jit(solution)/shard_map/all_to_all | solution.py:144
  49.8 0.1 fusion
  49.9 0.1 fusion.2
  50.0 0.1 fusion.1
  50.1 1.6 broadcast_in_dim.11
  51.7 0.0 copy-start.2
  51.7 0.0 copy-start
  51.7 10.5 %all-to-all-start.2 = ((bf16[8,2,16,8,512]{4,3,2,1,0:T(8,128)(2,1)}), bf16[8,2,16,8,512]{4,3,2,1,0:T(8,128)(2,1)}, u32[]{:S(2)}, u32[]{:S(2)}) async-start(bf16[8,2,16,8,512]{4,3,2,1,0:T(8,128)(2,1)} %broadcast_in_dim.11), calls=%async_computation.2 | async-start | bytes 4194304 | tf_op jit(solution)/shard_map/all_to_all | solution.py:153
  62.2 0.0 copy-done.2
  62.3 0.0 copy-start.5
  62.3 1.0 collective-permute-start.6
  63.3 1.8 collective-permute-start.4
  65.1 0.0 copy-done
  65.1 0.1 convert_element_type.14
  65.2 3.6 %collective-permute-start.8 = (bf16[256,1792]{1,0:T(8,128)(2,1)S(1)}, bf16[256,1792]{1,0:T(8,128)(2,1)S(1)}, u32[]{:S(2)}, u32[]{:S(2)}) collective-permute-start(bf16[256,1792]{1,0:T(8,128)(2,1)S(1)} %convert_element_type.14), channel_id=1, source_target_pairs={{0,8},{8,0},{1,9},{9,1},{2,10},{10,2},{3,11},{11,3},{4,12},{12,4},... | collective-permute-start | bytes 2752520 | tf_op jit(solution)/shard_map/ppermute | solution.py:23
  68.8 21.6 %collective-permute-done.6.refs_5_ = bf16[256,1792]{1,0:T(8,128)(2,1)S(1)} collective-permute-done((bf16[256,1792]{1,0:T(8,128)(2,1)S(1)}, bf16[256,1792]{1,0:T(8,128)(2,1)S(1)}, u32[]{:S(2)}, u32[]{:S(2)}) %collective-permute-start.6) | collective-permute-done | bytes 917536 | tf_op jit(solution)/shard_map/ppermute | solution.py:23
  90.3 0.0 copy-start.3
  90.4 0.0 copy-done.5
  90.4 0.9 collective-permute-start.7
  91.3 0.2 collective-permute-done.4.refs_2_
  91.5 0.0 copy-done.3
  91.5 0.0 copy-start.4
  91.5 0.9 copy-done.4
  92.4 1.7 collective-permute-start.5
  94.1 0.0 collective-permute-done.8
  94.1 1.9 %maximum_select_fusion.refs_6_ = bf16[512,1792]{1,0:T(8,128)(2,1)} fusion(bf16[256,1792]{1,0:T(8,128)(2,1)S(1)} %collective-permute-done.8, bf16[256,1792]{1,0:T(8,128)(2,1)S(1)} %convert_element_type.14, pred[]{:T(512)S(6)} %eq.36), kind=kLoop, calls=%fused_computation | loop fusion | flops 8257536 | bytes 3670017 | tf_op jit(solution)/shard_map/jit(_where)/select_n | solution.py:158
  96.0 8.0 %collective-permute-done.7.refs_4_ = bf16[128,1792]{1,0:T(8,128)(2,1)S(1)} collective-permute-done((bf16[128,1792]{1,0:T(8,128)(2,1)S(1)}, bf16[128,1792]{1,0:T(8,128)(2,1)S(1)}, u32[]{:S(2)}, u32[]{:S(2)}) %collective-permute-start.7) | collective-permute-done | bytes 458784 | tf_op jit(solution)/shard_map/ppermute | solution.py:23
  104.0 0.0 collective-permute-done.5.refs_3_
  104.0 0.8 copy-done.6
  104.8 9.1 %shard_map.84 = bf16[8,32,8,512]{3,2,1,0:T(8,128)(2,1)} custom-call(bf16[1024,1792]{1,0:T(8,128)(2,1)} %all-gather.2.cloned.1.call-done.refs_0_, bf16[256,1792]{1,0:T(8,128)(2,1)} %copy-done.5, bf16[256,1792]{1,0:T(8,128)(2,1)} %copy-done.4, bf16[128,1792]{1,0:T(8,128)(2,1)} %collective-permute-done.5.refs_3_, bf16[128,1792]{1,0:T(8,128)(2,1)} %copy-done.6, ...), custom_call_target="tpu_custom_call" | custom-call | flops 3758096384 | bytes 12582912 | tf_op jit(solution)/shard_map/pallas_call | solution.py:167
  113.9 0.0 all-to-all-done.2.refs_6_
  113.9 4.9 %all-to-all-start.3 = ((bf16[8,32,8,512]{3,2,1,0:T(8,128)(2,1)}), bf16[8,32,8,512]{3,2,1,0:T(8,128)(2,1)S(1)}, u32[]{:S(2)}, u32[]{:S(2)}) async-start(bf16[8,32,8,512]{3,2,1,0:T(8,128)(2,1)} %shard_map.84), calls=%async_computation.3 | async-start | bytes 4194304 | tf_op jit(solution)/shard_map/all_to_all | solution.py:176
  118.8 10.5 %shard_map.85 = (f32[256,1792]{1,0:T(8,128)}, f32[256,1792]{1,0:T(8,128)}) custom-call(bf16[1024,1792]{1,0:T(8,128)(2,1)} %all-gather.2.cloned.1.call-done.refs_0_, bf16[256,1792]{1,0:T(8,128)(2,1)} %copy-done.5, bf16[256,1792]{1,0:T(8,128)(2,1)} %copy-done.4, bf16[128,1792]{1,0:T(8,128)(2,1)} %collective-permute-done.5.refs_3_, ...), custom_call_target="tpu_custom_call" | custom-call | flops 3758096384 | bytes 12582912 | tf_op jit(solution)/shard_map/pallas_call | solution.py:178
  129.3 4.2 %collective-permute-start.9 = (f32[256,1792]{1,0:T(8,128)}, f32[256,1792]{1,0:T(8,128)}, u32[]{:S(2)}, u32[]{:S(2)}) collective-permute-start(f32[256,1792]{1,0:T(8,128)} %get-tuple-element.53), channel_id=1, source_target_pairs={{0,8},{8,0},{1,9},{9,1},{2,10},{10,2},{3,11},{11,3},{4,12},{12,4},... | collective-permute-start | bytes 5505032 | tf_op jit(solution)/shard_map/ppermute | solution.py:23
  133.5 0.1 stack.79.places_ref
  133.6 3.7 %collective-permute-done.9.other_ref = f32[256,1792]{1,0:T(8,128)} collective-permute-done((f32[256,1792]{1,0:T(8,128)}, f32[256,1792]{1,0:T(8,128)}, u32[]{:S(2)}, u32[]{:S(2)}) %collective-permute-start.9) | collective-permute-done | bytes 1835040 | tf_op jit(solution)/shard_map/ppermute | solution.py:23
  137.2 6.4 %shard_map.86 = (f32[256,1792]{1,0:T(8,128)}, f32[256,1792]{1,0:T(8,128)}, f32[256,1792]{1,0:T(8,128)}, f32[16,128]{1,0:T(8,128)}) custom-call(f32[256,1792]{1,0:T(8,128)} %get-tuple-element.52.grad_ref, f32[256,1792]{1,0:T(8,128)} %collective-permute-done.9.other_ref, f32[256,1792]{1,0:T(8,128)} %one_ref.1, f32[256,1792]{1,0:T(8,128)} %two_ref.1, ...), custom_call_target="tpu_custom_call" | custom-call | bytes 8388608 | tf_op jit(solution)/shard_map/pallas_call | solution.py:197
  143.6 0.4 all-to-all-done.3.got_ref
  144.0 0.8 shard_map.87
  144.8 0.0 copy-start.1
  144.8 5.9 %all-to-all-start.4 = ((f32[16,1,128]{2,1,0:T(1,128)}), f32[16,1,128]{2,1,0:T(1,128)S(1)}, u32[]{:S(2)}, u32[]{:S(2)}) async-start(f32[16,1,128]{2,1,0:T(1,128)} %bitcast.33), calls=%async_computation.4 | async-start | bytes 16384 | tf_op jit(solution)/shard_map/all_to_all | solution.py:208
  150.7 5.4 %all-to-all-done.4 = f32[16,1,128]{2,1,0:T(1,128)S(1)} async-done(((f32[16,1,128]{2,1,0:T(1,128)}), f32[16,1,128]{2,1,0:T(1,128)S(1)}, u32[]{:S(2)}, u32[]{:S(2)}) %all-to-all-start.4) | async-done | bytes 8224 | tf_op jit(solution)/shard_map/all_to_all | solution.py:208
  156.1 0.1 fusion.8
  156.2 23.6 %all_to_all.62 = bf16[16,24,512]{2,1,0:T(8,128)(2,1)S(1)} all-to-all(bf16[16,24,512]{2,1,0:T(8,128)(2,1)S(1)} %pad_maximum_fusion), channel_id=1, replica_groups=mesh['zh'=4,'y'=4,'c'=2,'zl'=2,'x'=4] {'zh','y'}, dimensions={0} | all-to-all | bytes 786432 | tf_op jit(solution)/shard_map/all_to_all | solution.py:212
  179.8 0.7 copy.34
  180.6 0.1 reduce_sum.27
  180.7 0.6 fusion.12
  182.7 0.0 copy-done.1
  182.7 1.3 broadcast_multiply_fusion
  (24 shorter events, 0.4 us)
Async XLA Ops:
  7.2 96.9 %all-gather.2.cloned.1.call-start = ((), (), s32[]{:S(2)}) async-start(), calls=%async_computation.6 | async-start | bytes 3899392 | tf_op jit(solution)/shard_map/all_gather | solution.py:137
  9.0 12.3 %all-to-all-start = ((bf16[8,16,1024]{2,1,0:T(8,128)(2,1)}), bf16[8,16,1024]{2,1,0:T(8,128)(2,1)S(1)}, u32[]{:S(2)}, u32[]{:S(2)}) async-start(bf16[8,16,1024]{2,1,0:T(8,128)(2,1)} %bitcast.68), calls=%async_computation | async-start | bytes 524288 | tf_op jit(solution)/shard_map/all_to_all | solution.py:141
  15.2 18.1 %collective-permute-start.1 = (bf16[64,1792]{1,0:T(8,128)(2,1)S(1)}, bf16[64,1792]{1,0:T(8,128)(2,1)S(1)}, u32[]{:S(2)}, u32[]{:S(2)}) collective-permute-start(bf16[64,1792]{1,0:T(8,128)(2,1)S(1)} %get-tuple-element.61), channel_id=1, source_target_pairs={{0,64},{64,128},{128,192},{192,0},{1,65},{65,129},{129,193},{193,1... | collective-permute-start | bytes 688136 | tf_op jit(solution)/shard_map/ppermute | solution.py:23
  18.2 15.1 %collective-permute-start = (bf16[64,1792]{1,0:T(8,128)(2,1)S(1)}, bf16[64,1792]{1,0:T(8,128)(2,1)S(1)}, u32[]{:S(2)}, u32[]{:S(2)}) collective-permute-start(bf16[64,1792]{1,0:T(8,128)(2,1)S(1)} %get-tuple-element.61), channel_id=1, source_target_pairs={{0,192},{64,0},{128,64},{192,128},{1,193},{65,1},{129,65},{193,129... | collective-permute-start | bytes 688136 | tf_op jit(solution)/shard_map/ppermute | solution.py:23
  34.1 15.7 %all-to-all-start.1 = ((bf16[16,16,512]{2,0,1:T(8,128)(2,1)}), bf16[16,16,512]{2,0,1:T(8,128)(2,1)S(1)}, u32[]{:S(2)}, u32[]{:S(2)}) async-start(bf16[16,16,512]{2,0,1:T(8,128)(2,1)} %bitcast.58), calls=%async_computation.1 | async-start | bytes 524288 | tf_op jit(solution)/shard_map/all_to_all | solution.py:144
  39.4 8.1 %collective-permute-start.3 = (bf16[32,1792]{1,0:T(8,128)(2,1)S(1)}, bf16[32,1792]{1,0:T(8,128)(2,1)S(1)}, u32[]{:S(2)}, u32[]{:S(2)}) collective-permute-start(bf16[32,1792]{1,0:T(8,128)(2,1)S(1)} %slice.44), channel_id=1, source_target_pairs={{0,64},{64,128},{128,192},{192,0},{1,65},{65,129},{129,193},{193,1... | collective-permute-start | bytes 344072 | tf_op jit(solution)/shard_map/ppermute | solution.py:23
  41.7 5.7 %collective-permute-start.2 = (bf16[32,1792]{1,0:T(8,128)(2,1)S(1)}, bf16[32,1792]{1,0:T(8,128)(2,1)S(1)}, u32[]{:S(2)}, u32[]{:S(2)}) collective-permute-start(bf16[32,1792]{1,0:T(8,128)(2,1)S(1)} %slice.43), channel_id=1, source_target_pairs={{0,192},{64,0},{128,64},{192,128},{1,193},{65,1},{129,65},{193,129... | collective-permute-start | bytes 344072 | tf_op jit(solution)/shard_map/ppermute | solution.py:23
  51.7 10.5 %copy-start.2 = (bf16[128,1792]{1,0:T(8,128)(2,1)S(1)}, bf16[128,1792]{1,0:T(8,128)(2,1)}, u32[]{:S(2)}) copy-start(bf16[128,1792]{1,0:T(8,128)(2,1)} %param.6) | copy-start | bytes 1376260
  51.7 13.3 %copy-start = (f32[256,1792]{1,0:T(8,128)S(1)}, f32[256,1792]{1,0:T(8,128)}, u32[]{:S(2)}) copy-start(f32[256,1792]{1,0:T(8,128)} %master_ref.1) | copy-start | bytes 5505028
  51.7 62.2 %all-to-all-start.2 = ((bf16[8,2,16,8,512]{4,3,2,1,0:T(8,128)(2,1)}), bf16[8,2,16,8,512]{4,3,2,1,0:T(8,128)(2,1)}, u32[]{:S(2)}, u32[]{:S(2)}) async-start(bf16[8,2,16,8,512]{4,3,2,1,0:T(8,128)(2,1)} %broadcast_in_dim.11), calls=%async_computation.2 | async-start | bytes 4194304 | tf_op jit(solution)/shard_map/all_to_all | solution.py:153
  62.3 28.1 %copy-start.5 = (bf16[256,1792]{1,0:T(8,128)(2,1)}, bf16[256,1792]{1,0:T(8,128)(2,1)S(1)}, u32[]{:S(2)}) copy-start(bf16[256,1792]{1,0:T(8,128)(2,1)S(1)} %constant_dynamic-update-slice_fusion.refs_1_) | copy-start | bytes 2752516
  62.3 28.0 %collective-permute-start.6 = (bf16[256,1792]{1,0:T(8,128)(2,1)S(1)}, bf16[256,1792]{1,0:T(8,128)(2,1)S(1)}, u32[]{:S(2)}, u32[]{:S(2)}) collective-permute-start(bf16[256,1792]{1,0:T(8,128)(2,1)S(1)} %constant_dynamic-update-slice_fusion.refs_1_), channel_id=1, source_target_pairs={{0,16},{16,32},{32,48},{48,0},{1,17},{17,33},{33,49},{49,1},{2,18}... | collective-permute-start | bytes 2752520 | tf_op jit(solution)/shard_map/ppermute | solution.py:23
  63.3 28.2 %collective-permute-start.4 = (bf16[256,1792]{1,0:T(8,128)(2,1)S(1)}, bf16[256,1792]{1,0:T(8,128)(2,1)S(1)}, u32[]{:S(2)}, u32[]{:S(2)}) collective-permute-start(bf16[256,1792]{1,0:T(8,128)(2,1)S(1)} %constant_dynamic-update-slice_fusion.refs_1_), channel_id=1, source_target_pairs={{0,48},{16,0},{32,16},{48,32},{1,49},{17,1},{33,17},{49,33},{2,50}... | collective-permute-start | bytes 2752520 | tf_op jit(solution)/shard_map/ppermute | solution.py:23
  65.2 28.9 %collective-permute-start.8 = (bf16[256,1792]{1,0:T(8,128)(2,1)S(1)}, bf16[256,1792]{1,0:T(8,128)(2,1)S(1)}, u32[]{:S(2)}, u32[]{:S(2)}) collective-permute-start(bf16[256,1792]{1,0:T(8,128)(2,1)S(1)} %convert_element_type.14), channel_id=1, source_target_pairs={{0,8},{8,0},{1,9},{9,1},{2,10},{10,2},{3,11},{11,3},{4,12},{12,4},... | collective-permute-start | bytes 2752520 | tf_op jit(solution)/shard_map/ppermute | solution.py:23
  90.3 1.1 copy-start.3
  90.4 13.6 %collective-permute-start.7 = (bf16[128,1792]{1,0:T(8,128)(2,1)S(1)}, bf16[128,1792]{1,0:T(8,128)(2,1)S(1)}, u32[]{:S(2)}, u32[]{:S(2)}) collective-permute-start(bf16[128,1792]{1,0:T(8,128)(2,1)S(1)} %slice.58), channel_id=1, source_target_pairs={{0,16},{16,32},{32,48},{48,0},{1,17},{17,33},{33,49},{49,1},{2,18}... | collective-permute-start | bytes 1376264 | tf_op jit(solution)/shard_map/ppermute | solution.py:23
  91.5 0.9 copy-start.4
  92.4 11.6 %collective-permute-start.5 = (bf16[128,1792]{1,0:T(8,128)(2,1)S(1)}, bf16[128,1792]{1,0:T(8,128)(2,1)}, u32[]{:S(2)}, u32[]{:S(2)}) collective-permute-start(bf16[128,1792]{1,0:T(8,128)(2,1)S(1)} %slice.57), channel_id=1, source_target_pairs={{0,48},{16,0},{32,16},{48,32},{1,49},{17,1},{33,17},{49,33},{2,50}... | collective-permute-start | bytes 1376264 | tf_op jit(solution)/shard_map/ppermute | solution.py:23
  104.0 0.8 copy-start.6
  113.9 30.0 %all-to-all-start.3 = ((bf16[8,32,8,512]{3,2,1,0:T(8,128)(2,1)}), bf16[8,32,8,512]{3,2,1,0:T(8,128)(2,1)S(1)}, u32[]{:S(2)}, u32[]{:S(2)}) async-start(bf16[8,32,8,512]{3,2,1,0:T(8,128)(2,1)} %shard_map.84), calls=%async_computation.3 | async-start | bytes 4194304 | tf_op jit(solution)/shard_map/all_to_all | solution.py:176
  129.3 7.9 %collective-permute-start.9 = (f32[256,1792]{1,0:T(8,128)}, f32[256,1792]{1,0:T(8,128)}, u32[]{:S(2)}, u32[]{:S(2)}) collective-permute-start(f32[256,1792]{1,0:T(8,128)} %get-tuple-element.53), channel_id=1, source_target_pairs={{0,8},{8,0},{1,9},{9,1},{2,10},{10,2},{3,11},{11,3},{4,12},{12,4},... | collective-permute-start | bytes 5505032 | tf_op jit(solution)/shard_map/ppermute | solution.py:23
  144.8 38.0 %copy-start.1 = (f32[256,1792]{1,0:T(8,128)S(1)}, f32[256,1792]{1,0:T(8,128)}, u32[]{:S(2)}) copy-start(f32[256,1792]{1,0:T(8,128)} %get-tuple-element.57) | copy-start | bytes 5505028
  144.8 11.3 %all-to-all-start.4 = ((f32[16,1,128]{2,1,0:T(1,128)}), f32[16,1,128]{2,1,0:T(1,128)S(1)}, u32[]{:S(2)}, u32[]{:S(2)}) async-start(f32[16,1,128]{2,1,0:T(1,128)} %bitcast.33), calls=%async_computation.4 | async-start | bytes 16384 | tf_op jit(solution)/shard_map/all_to_all | solution.py:208
Sparse Core Ops, SparseCore 0:
  11.0 91.1 all-gather.1

commit v2 on v1

--- a/solution.py
+++ b/solution.py
@@ -83,7 +83,7 @@
         copy.wait()
     grad = dot(jnp.concatenate(feats, 0), tokens_ref[...], 0, 0)
     grad_ref[...] = grad[:256]
-    grad_other_ref[...] = grad[256:]
+    grad_other_ref[...] = grad[256:].astype(BF)
 
 
 def place_kernel(places_ref, got_ref, out_ref):
@@ -101,7 +101,7 @@
     def _():
         acc_ref[...] = jnp.zeros_like(acc_ref)
 
-    grad = grad_ref[...] + other_ref[...]
+    grad = grad_ref[...] + other_ref[...].astype(F32)
     master = master_ref[...]
     new_one = beta_one * one_ref[...] + (1.0 - beta_one) * grad
     new_two = beta_two * two_ref[...] + (1.0 - beta_two) * grad * grad
@@ -179,7 +179,7 @@
         grad_kernel,
         in_specs=[anywhere] * 6 + [vmem],
         out_specs=[vmem] * 2,
-        out_shape=[f32] * 2,
+        out_shape=[f32, jax.ShapeDtypeStruct((256, 1792), BF)],
         scratch_shapes=scratch,
         compiler_params=limit,
         cost_estimate=cost(2 * 2048 * 512 * 1792, 12 << 20),

time: 192 us -> 190 us (0.990)
  starting transfers between devices: 54.7 us -> 52.1 us
  waiting for transfers between devices: 58.7 us -> 61.1 us
    ppermute x10, waiting for transfers between devices: 49.8 us -> 52.1 us  [shift(): lax.ppermute(value, axis, [(i, (i - by) % size) for i in range(size)])]
  transfers between devices with their start and end apart: 16 -> 16, of which waited for: 10 -> 11; matrix products, arithmetic and copies ran while one was open for 3% -> 3% of each run, Pallas kernels for 14% -> 13%
where the time goes in v2:
time: 190 us
  waiting for transfers between devices  61.1 us (32%)
  starting transfers between devices  52.1 us (27%)
  Pallas kernels  26.3 us (14%)
  blocking collectives  21.8 us (11%)
  between operations  15.6 us (8%)
  local copies, waits for them, and re-layouts  8.7 us (5%)
  other arithmetic  3.9 us (2%)
    ppermute x10, waiting for transfers between devices, shift(): lax.ppermute(value, axis, [(i, (i - by) % size) for i in range(size)])  52.1 us
    all_to_all x1, blocking collectives, on_device(): out = lax.all_to_all(out, CH, split_axis=0, concat_axis=0, tiled=True)  21.8 us
    ppermute x10, starting transfers between devices, shift(): lax.ppermute(value, axis, [(i, (i - by) % size) for i in range(size)])  20.5 us
    pallas_call x1, Pallas kernels, on_device(): pl.pallas_call(grad_kernel, in_specs=[anywhere] * 6 + [vmem], out_specs=[...  10.3 us
    all_to_all x1, starting transfers between devices, on_device(): feats = lax.all_to_all(copies, TP, split_axis=0, concat_axis=0, tiled=True)  10.2 us
    pallas_call x1, Pallas kernels, on_device(): pl.pallas_call(part_kernel, in_specs=[anywhere] * 6 + [vmem], out_specs=v...  9.11 us
    all_to_all x1, starting transfers between devices, on_device(): lax.all_to_all(activations, TP, split_axis=0, concat_axis=1, tiled=True)  6.22 us
    pallas_call x1, Pallas kernels, on_device(): pl.pallas_call(last_kernel, grid=(2,), in_specs=[slab] * 5, out_specs=[sl...  6.1 us
  transfers between devices with their start and end apart: 16, of which 11 were waited for; matrix products, arithmetic and copies ran while one was open for 3% of the time, Pallas kernels for 13%

profile of v2, /device:TPU:1, one launch (start us, length us, event | category | flops | bytes accessed | tf_op | source)
XLA Modules:
  0.0 189.5 jit_solution(11026890665513734654)
XLA Ops:
  7.2 0.0 all-gather.2.cloned.1.call-start
  7.2 1.8 slice_bitcast_fusion.1
  9.0 0.0 all-gather.2.cloned.1.call-update
  9.0 6.2 %all-to-all-start = ((bf16[8,16,1024]{2,1,0:T(8,128)(2,1)}), bf16[8,16,1024]{2,1,0:T(8,128)(2,1)S(1)}, u32[]{:S(2)}, u32[]{:S(2)}) async-start(bf16[8,16,1024]{2,1,0:T(8,128)(2,1)} %bitcast.68), calls=%async_computation | async-start | bytes 524288 | tf_op jit(solution)/shard_map/all_to_all | solution.py:141
  15.2 3.0 %collective-permute-start.1 = (bf16[64,1792]{1,0:T(8,128)(2,1)S(1)}, bf16[64,1792]{1,0:T(8,128)(2,1)S(1)}, u32[]{:S(2)}, u32[]{:S(2)}) collective-permute-start(bf16[64,1792]{1,0:T(8,128)(2,1)S(1)} %get-tuple-element.61), channel_id=1, source_target_pairs={{0,64},{64,128},{128,192},{192,0},{1,65},{65,129},{129,193},{193,1... | collective-permute-start | bytes 688136 | tf_op jit(solution)/shard_map/ppermute | solution.py:23
  18.2 2.2 %collective-permute-start = (bf16[64,1792]{1,0:T(8,128)(2,1)S(1)}, bf16[64,1792]{1,0:T(8,128)(2,1)S(1)}, u32[]{:S(2)}, u32[]{:S(2)}) collective-permute-start(bf16[64,1792]{1,0:T(8,128)(2,1)S(1)} %get-tuple-element.61), channel_id=1, source_target_pairs={{0,192},{64,0},{128,64},{192,128},{1,193},{65,1},{129,65},{193,129... | collective-permute-start | bytes 688136 | tf_op jit(solution)/shard_map/ppermute | solution.py:23
  20.4 0.9 all-to-all-done
  21.3 12.8 %collective-permute-done.1 = bf16[64,1792]{1,0:T(8,128)(2,1)S(1)} collective-permute-done((bf16[64,1792]{1,0:T(8,128)(2,1)S(1)}, bf16[64,1792]{1,0:T(8,128)(2,1)S(1)}, u32[]{:S(2)}, u32[]{:S(2)}) %collective-permute-start.1) | collective-permute-done | bytes 229408 | tf_op jit(solution)/shard_map/ppermute | solution.py:23
  34.2 0.0 collective-permute-done
  34.2 0.7 copy.36
  34.9 5.1 %all-to-all-start.1 = ((bf16[16,16,512]{2,0,1:T(8,128)(2,1)}), bf16[16,16,512]{2,0,1:T(8,128)(2,1)S(1)}, u32[]{:S(2)}, u32[]{:S(2)}) async-start(bf16[16,16,512]{2,0,1:T(8,128)(2,1)} %bitcast.58), calls=%async_computation.1 | async-start | bytes 524288 | tf_op jit(solution)/shard_map/all_to_all | solution.py:144
  40.1 2.3 %collective-permute-start.3 = (bf16[32,1792]{1,0:T(8,128)(2,1)S(1)}, bf16[32,1792]{1,0:T(8,128)(2,1)S(1)}, u32[]{:S(2)}, u32[]{:S(2)}) collective-permute-start(bf16[32,1792]{1,0:T(8,128)(2,1)S(1)} %slice.44), channel_id=1, source_target_pairs={{0,64},{64,128},{128,192},{192,0},{1,65},{65,129},{129,193},{193,1... | collective-permute-start | bytes 344072 | tf_op jit(solution)/shard_map/ppermute | solution.py:23
  42.4 1.3 collective-permute-start.2
  43.7 4.1 %collective-permute-done.3 = bf16[32,1792]{1,0:T(8,128)(2,1)S(1)} collective-permute-done((bf16[32,1792]{1,0:T(8,128)(2,1)S(1)}, bf16[32,1792]{1,0:T(8,128)(2,1)S(1)}, u32[]{:S(2)}, u32[]{:S(2)}) %collective-permute-start.3) | collective-permute-done | bytes 114720 | tf_op jit(solution)/shard_map/ppermute | solution.py:23
  47.8 1.9 %collective-permute-done.2 = bf16[32,1792]{1,0:T(8,128)(2,1)S(1)} collective-permute-done((bf16[32,1792]{1,0:T(8,128)(2,1)S(1)}, bf16[32,1792]{1,0:T(8,128)(2,1)S(1)}, u32[]{:S(2)}, u32[]{:S(2)}) %collective-permute-start.2) | collective-permute-done | bytes 114720 | tf_op jit(solution)/shard_map/ppermute | solution.py:23
  49.7 0.5 all-to-all-done.1
  50.3 0.1 fusion
  50.4 0.1 fusion.2
  50.5 0.1 fusion.1
  50.6 1.6 broadcast_in_dim.11
  52.2 0.0 copy-start
  52.2 10.2 %all-to-all-start.2 = ((bf16[8,2,16,8,512]{4,3,2,1,0:T(8,128)(2,1)}), bf16[8,2,16,8,512]{4,3,2,1,0:T(8,128)(2,1)}, u32[]{:S(2)}, u32[]{:S(2)}) async-start(bf16[8,2,16,8,512]{4,3,2,1,0:T(8,128)(2,1)} %broadcast_in_dim.11), calls=%async_computation.2 | async-start | bytes 4194304 | tf_op jit(solution)/shard_map/all_to_all | solution.py:153
  62.4 0.0 copy-done.2
  62.5 0.0 copy-start.6
  62.5 1.0 collective-permute-start.6
  63.6 1.7 collective-permute-start.4
  65.3 0.0 copy-done
  65.3 0.1 convert_element_type.14
  65.4 3.3 %collective-permute-start.8 = (bf16[256,1792]{1,0:T(8,128)(2,1)S(1)}, bf16[256,1792]{1,0:T(8,128)(2,1)S(1)}, u32[]{:S(2)}, u32[]{:S(2)}) collective-permute-start(bf16[256,1792]{1,0:T(8,128)(2,1)S(1)} %convert_element_type.14), channel_id=1, source_target_pairs={{0,8},{8,0},{1,9},{9,1},{2,10},{10,2},{3,11},{11,3},{4,12},{12,4},... | collective-permute-start | bytes 2752520 | tf_op jit(solution)/shard_map/ppermute | solution.py:23
  68.7 24.8 %collective-permute-done.6.refs_5_ = bf16[256,1792]{1,0:T(8,128)(2,1)S(1)} collective-permute-done((bf16[256,1792]{1,0:T(8,128)(2,1)S(1)}, bf16[256,1792]{1,0:T(8,128)(2,1)S(1)}, u32[]{:S(2)}, u32[]{:S(2)}) %collective-permute-start.6) | collective-permute-done | bytes 917536 | tf_op jit(solution)/shard_map/ppermute | solution.py:23
  93.5 0.0 copy-start.4
  93.5 0.0 copy-done.6
  93.5 0.1 collective-permute-start.7
  93.6 0.0 collective-permute-done.4.refs_2_
  93.6 0.8 copy-done.4
  94.4 0.0 copy-start.5
  94.5 0.9 copy-done.5
  95.3 1.9 collective-permute-start.5
  97.2 0.0 collective-permute-done.8
  97.2 1.9 %maximum_select_fusion.refs_6_ = bf16[512,1792]{1,0:T(8,128)(2,1)} fusion(bf16[256,1792]{1,0:T(8,128)(2,1)S(1)} %collective-permute-done.8, bf16[256,1792]{1,0:T(8,128)(2,1)S(1)} %convert_element_type.14, pred[]{:T(512)S(6)} %eq.36), kind=kLoop, calls=%fused_computation | loop fusion | flops 8257536 | bytes 3670017 | tf_op jit(solution)/shard_map/jit(_where)/select_n | solution.py:158
  99.2 5.8 %collective-permute-done.7.refs_4_ = bf16[128,1792]{1,0:T(8,128)(2,1)S(1)} collective-permute-done((bf16[128,1792]{1,0:T(8,128)(2,1)S(1)}, bf16[128,1792]{1,0:T(8,128)(2,1)S(1)}, u32[]{:S(2)}, u32[]{:S(2)}) %collective-permute-start.7) | collective-permute-done | bytes 458784 | tf_op jit(solution)/shard_map/ppermute | solution.py:23
  105.0 0.5 collective-permute-done.5.refs_3_
  105.5 0.3 copy-done.7
  105.7 9.1 %shard_map.84 = bf16[8,32,8,512]{3,2,1,0:T(8,128)(2,1)} custom-call(bf16[1024,1792]{1,0:T(8,128)(2,1)} %all-gather.2.cloned.1.call-done.refs_0_, bf16[256,1792]{1,0:T(8,128)(2,1)} %copy-done.6, bf16[256,1792]{1,0:T(8,128)(2,1)} %copy-done.5, bf16[128,1792]{1,0:T(8,128)(2,1)} %collective-permute-done.5.refs_3_, bf16[128,1792]{1,0:T(8,128)(2,1)} %copy-done.7, ...), custom_call_target="tpu_custom_call" | custom-call | flops 3758096384 | bytes 12582912 | tf_op jit(solution)/shard_map/pallas_call | solution.py:167
  114.9 0.0 all-to-all-done.2.refs_6_
  114.9 4.6 %all-to-all-start.3 = ((bf16[8,32,8,512]{3,2,1,0:T(8,128)(2,1)}), bf16[8,32,8,512]{3,2,1,0:T(8,128)(2,1)S(1)}, u32[]{:S(2)}, u32[]{:S(2)}) async-start(bf16[8,32,8,512]{3,2,1,0:T(8,128)(2,1)} %shard_map.84), calls=%async_computation.3 | async-start | bytes 4194304 | tf_op jit(solution)/shard_map/all_to_all | solution.py:176
  119.5 10.3 %shard_map.85 = (f32[256,1792]{1,0:T(8,128)}, bf16[256,1792]{1,0:T(8,128)(2,1)}) custom-call(bf16[1024,1792]{1,0:T(8,128)(2,1)} %all-gather.2.cloned.1.call-done.refs_0_, bf16[256,1792]{1,0:T(8,128)(2,1)} %copy-done.6, bf16[256,1792]{1,0:T(8,128)(2,1)} %copy-done.5, bf16[128,1792]{1,0:T(8,128)(2,1)} %collective-permute-done.5.refs_3_, ...), custom_call_target="tpu_custom_call" | custom-call | flops 3758096384 | bytes 12582912 | tf_op jit(solution)/shard_map/pallas_call | solution.py:178
  129.8 3.6 %collective-permute-start.9 = (bf16[256,1792]{1,0:T(8,128)(2,1)}, bf16[256,1792]{1,0:T(8,128)(2,1)S(1)}, u32[]{:S(2)}, u32[]{:S(2)}) collective-permute-start(bf16[256,1792]{1,0:T(8,128)(2,1)} %get-tuple-element.53), channel_id=1, source_target_pairs={{0,8},{8,0},{1,9},{9,1},{2,10},{10,2},{3,11},{11,3},{4,12},{12,4},... | collective-permute-start | bytes 2752520 | tf_op jit(solution)/shard_map/ppermute | solution.py:23
  133.4 0.1 stack.79.places_ref
  133.5 2.2 %collective-permute-done.9.other_ref = bf16[256,1792]{1,0:T(8,128)(2,1)S(1)} collective-permute-done((bf16[256,1792]{1,0:T(8,128)(2,1)}, bf16[256,1792]{1,0:T(8,128)(2,1)S(1)}, u32[]{:S(2)}, u32[]{:S(2)}) %collective-permute-start.9) | collective-permute-done | bytes 917536 | tf_op jit(solution)/shard_map/ppermute | solution.py:23
  135.7 0.9 copy-done.3
  136.6 6.1 %shard_map.86 = (f32[256,1792]{1,0:T(8,128)}, f32[256,1792]{1,0:T(8,128)}, f32[256,1792]{1,0:T(8,128)}, f32[16,128]{1,0:T(8,128)}) custom-call(f32[256,1792]{1,0:T(8,128)} %get-tuple-element.52.grad_ref, bf16[256,1792]{1,0:T(8,128)(2,1)} %copy-done.3, f32[256,1792]{1,0:T(8,128)} %one_ref.1, f32[256,1792]{1,0:T(8,128)} %two_ref.1, f32[256,1792]{1,0:T(8,128)} %master_ref.1), custom_call_target="tpu_custom_call" | custom-call | bytes 8388608 | tf_op jit(solution)/shard_map/pallas_call | solution.py:197
  142.7 2.2 %all-to-all-done.3.got_ref = bf16[8,32,8,512]{3,2,1,0:T(8,128)(2,1)S(1)} async-done(((bf16[8,32,8,512]{3,2,1,0:T(8,128)(2,1)}), bf16[8,32,8,512]{3,2,1,0:T(8,128)(2,1)S(1)}, u32[]{:S(2)}, u32[]{:S(2)}) %all-to-all-start.3) | async-done | bytes 2097184 | tf_op jit(solution)/shard_map/all_to_all | solution.py:176
  144.9 0.8 shard_map.87
  145.7 0.0 copy-start.1
  145.7 5.4 %all-to-all-start.4 = ((f32[16,1,128]{2,1,0:T(1,128)}), f32[16,1,128]{2,1,0:T(1,128)S(1)}, u32[]{:S(2)}, u32[]{:S(2)}) async-start(f32[16,1,128]{2,1,0:T(1,128)} %bitcast.33), calls=%async_computation.4 | async-start | bytes 16384 | tf_op jit(solution)/shard_map/all_to_all | solution.py:208
  151.1 5.4 %all-to-all-done.4 = f32[16,1,128]{2,1,0:T(1,128)S(1)} async-done(((f32[16,1,128]{2,1,0:T(1,128)}), f32[16,1,128]{2,1,0:T(1,128)S(1)}, u32[]{:S(2)}, u32[]{:S(2)}) %all-to-all-start.4) | async-done | bytes 8224 | tf_op jit(solution)/shard_map/all_to_all | solution.py:208
  156.6 0.1 fusion.8
  156.7 21.8 %all_to_all.62 = bf16[16,24,512]{2,1,0:T(8,128)(2,1)S(1)} all-to-all(bf16[16,24,512]{2,1,0:T(8,128)(2,1)S(1)} %pad_maximum_fusion), channel_id=1, replica_groups=mesh['zh'=4,'y'=4,'c'=2,'zl'=2,'x'=4] {'zh','y'}, dimensions={0} | all-to-all | bytes 786432 | tf_op jit(solution)/shard_map/all_to_all | solution.py:212
  178.5 0.7 copy.34
  179.3 0.1 reduce_sum.27
  179.4 0.6 fusion.12
  181.3 0.0 copy-done.1
  181.3 1.3 broadcast_multiply_fusion
  (26 shorter events, 0.4 us)
Async XLA Ops:
  7.2 98.3 %all-gather.2.cloned.1.call-start = ((), (), s32[]{:S(2)}) async-start(), calls=%async_computation.6 | async-start | bytes 3899392 | tf_op jit(solution)/shard_map/all_gather | solution.py:137
  9.0 12.3 %all-to-all-start = ((bf16[8,16,1024]{2,1,0:T(8,128)(2,1)}), bf16[8,16,1024]{2,1,0:T(8,128)(2,1)S(1)}, u32[]{:S(2)}, u32[]{:S(2)}) async-start(bf16[8,16,1024]{2,1,0:T(8,128)(2,1)} %bitcast.68), calls=%async_computation | async-start | bytes 524288 | tf_op jit(solution)/shard_map/all_to_all | solution.py:141
  15.2 19.0 %collective-permute-start.1 = (bf16[64,1792]{1,0:T(8,128)(2,1)S(1)}, bf16[64,1792]{1,0:T(8,128)(2,1)S(1)}, u32[]{:S(2)}, u32[]{:S(2)}) collective-permute-start(bf16[64,1792]{1,0:T(8,128)(2,1)S(1)} %get-tuple-element.61), channel_id=1, source_target_pairs={{0,64},{64,128},{128,192},{192,0},{1,65},{65,129},{129,193},{193,1... | collective-permute-start | bytes 688136 | tf_op jit(solution)/shard_map/ppermute | solution.py:23
  18.2 16.0 %collective-permute-start = (bf16[64,1792]{1,0:T(8,128)(2,1)S(1)}, bf16[64,1792]{1,0:T(8,128)(2,1)S(1)}, u32[]{:S(2)}, u32[]{:S(2)}) collective-permute-start(bf16[64,1792]{1,0:T(8,128)(2,1)S(1)} %get-tuple-element.61), channel_id=1, source_target_pairs={{0,192},{64,0},{128,64},{192,128},{1,193},{65,1},{129,65},{193,129... | collective-permute-start | bytes 688136 | tf_op jit(solution)/shard_map/ppermute | solution.py:23
  34.9 15.3 %all-to-all-start.1 = ((bf16[16,16,512]{2,0,1:T(8,128)(2,1)}), bf16[16,16,512]{2,0,1:T(8,128)(2,1)S(1)}, u32[]{:S(2)}, u32[]{:S(2)}) async-start(bf16[16,16,512]{2,0,1:T(8,128)(2,1)} %bitcast.58), calls=%async_computation.1 | async-start | bytes 524288 | tf_op jit(solution)/shard_map/all_to_all | solution.py:144
  40.1 7.7 %collective-permute-start.3 = (bf16[32,1792]{1,0:T(8,128)(2,1)S(1)}, bf16[32,1792]{1,0:T(8,128)(2,1)S(1)}, u32[]{:S(2)}, u32[]{:S(2)}) collective-permute-start(bf16[32,1792]{1,0:T(8,128)(2,1)S(1)} %slice.44), channel_id=1, source_target_pairs={{0,64},{64,128},{128,192},{192,0},{1,65},{65,129},{129,193},{193,1... | collective-permute-start | bytes 344072 | tf_op jit(solution)/shard_map/ppermute | solution.py:23
  42.4 7.3 %collective-permute-start.2 = (bf16[32,1792]{1,0:T(8,128)(2,1)S(1)}, bf16[32,1792]{1,0:T(8,128)(2,1)S(1)}, u32[]{:S(2)}, u32[]{:S(2)}) collective-permute-start(bf16[32,1792]{1,0:T(8,128)(2,1)S(1)} %slice.43), channel_id=1, source_target_pairs={{0,192},{64,0},{128,64},{192,128},{1,193},{65,1},{129,65},{193,129... | collective-permute-start | bytes 344072 | tf_op jit(solution)/shard_map/ppermute | solution.py:23
  52.2 10.2 %copy-start.2 = (bf16[128,1792]{1,0:T(8,128)(2,1)S(1)}, bf16[128,1792]{1,0:T(8,128)(2,1)}, u32[]{:S(2)}) copy-start(bf16[128,1792]{1,0:T(8,128)(2,1)} %param.6) | copy-start | bytes 1376260
  52.2 13.1 %copy-start = (f32[256,1792]{1,0:T(8,128)S(1)}, f32[256,1792]{1,0:T(8,128)}, u32[]{:S(2)}) copy-start(f32[256,1792]{1,0:T(8,128)} %master_ref.1) | copy-start | bytes 5505028
  52.2 62.7 %all-to-all-start.2 = ((bf16[8,2,16,8,512]{4,3,2,1,0:T(8,128)(2,1)}), bf16[8,2,16,8,512]{4,3,2,1,0:T(8,128)(2,1)}, u32[]{:S(2)}, u32[]{:S(2)}) async-start(bf16[8,2,16,8,512]{4,3,2,1,0:T(8,128)(2,1)} %broadcast_in_dim.11), calls=%async_computation.2 | async-start | bytes 4194304 | tf_op jit(solution)/shard_map/all_to_all | solution.py:153
  62.5 31.0 %copy-start.6 = (bf16[256,1792]{1,0:T(8,128)(2,1)}, bf16[256,1792]{1,0:T(8,128)(2,1)S(1)}, u32[]{:S(2)}) copy-start(bf16[256,1792]{1,0:T(8,128)(2,1)S(1)} %constant_dynamic-update-slice_fusion.refs_1_) | copy-start | bytes 2752516
  62.5 31.0 %collective-permute-start.6 = (bf16[256,1792]{1,0:T(8,128)(2,1)S(1)}, bf16[256,1792]{1,0:T(8,128)(2,1)S(1)}, u32[]{:S(2)}, u32[]{:S(2)}) collective-permute-start(bf16[256,1792]{1,0:T(8,128)(2,1)S(1)} %constant_dynamic-update-slice_fusion.refs_1_), channel_id=1, source_target_pairs={{0,16},{16,32},{32,48},{48,0},{1,17},{17,33},{33,49},{49,1},{2,18}... | collective-permute-start | bytes 2752520 | tf_op jit(solution)/shard_map/ppermute | solution.py:23
  63.6 30.1 %collective-permute-start.4 = (bf16[256,1792]{1,0:T(8,128)(2,1)S(1)}, bf16[256,1792]{1,0:T(8,128)(2,1)S(1)}, u32[]{:S(2)}, u32[]{:S(2)}) collective-permute-start(bf16[256,1792]{1,0:T(8,128)(2,1)S(1)} %constant_dynamic-update-slice_fusion.refs_1_), channel_id=1, source_target_pairs={{0,48},{16,0},{32,16},{48,32},{1,49},{17,1},{33,17},{49,33},{2,50}... | collective-permute-start | bytes 2752520 | tf_op jit(solution)/shard_map/ppermute | solution.py:23
  65.4 31.8 %collective-permute-start.8 = (bf16[256,1792]{1,0:T(8,128)(2,1)S(1)}, bf16[256,1792]{1,0:T(8,128)(2,1)S(1)}, u32[]{:S(2)}, u32[]{:S(2)}) collective-permute-start(bf16[256,1792]{1,0:T(8,128)(2,1)S(1)} %convert_element_type.14), channel_id=1, source_target_pairs={{0,8},{8,0},{1,9},{9,1},{2,10},{10,2},{3,11},{11,3},{4,12},{12,4},... | collective-permute-start | bytes 2752520 | tf_op jit(solution)/shard_map/ppermute | solution.py:23
  93.5 0.9 copy-start.4
  93.5 11.4 %collective-permute-start.7 = (bf16[128,1792]{1,0:T(8,128)(2,1)S(1)}, bf16[128,1792]{1,0:T(8,128)(2,1)S(1)}, u32[]{:S(2)}, u32[]{:S(2)}) collective-permute-start(bf16[128,1792]{1,0:T(8,128)(2,1)S(1)} %slice.58), channel_id=1, source_target_pairs={{0,16},{16,32},{32,48},{48,0},{1,17},{17,33},{33,49},{49,1},{2,18}... | collective-permute-start | bytes 1376264 | tf_op jit(solution)/shard_map/ppermute | solution.py:23
  94.4 0.9 copy-start.5
  95.3 10.1 %collective-permute-start.5 = (bf16[128,1792]{1,0:T(8,128)(2,1)S(1)}, bf16[128,1792]{1,0:T(8,128)(2,1)}, u32[]{:S(2)}, u32[]{:S(2)}) collective-permute-start(bf16[128,1792]{1,0:T(8,128)(2,1)S(1)} %slice.57), channel_id=1, source_target_pairs={{0,48},{16,0},{32,16},{48,32},{1,49},{17,1},{33,17},{49,33},{2,50}... | collective-permute-start | bytes 1376264 | tf_op jit(solution)/shard_map/ppermute | solution.py:23
  105.0 0.8 copy-start.7
  114.9 30.0 %all-to-all-start.3 = ((bf16[8,32,8,512]{3,2,1,0:T(8,128)(2,1)}), bf16[8,32,8,512]{3,2,1,0:T(8,128)(2,1)S(1)}, u32[]{:S(2)}, u32[]{:S(2)}) async-start(bf16[8,32,8,512]{3,2,1,0:T(8,128)(2,1)} %shard_map.84), calls=%async_computation.3 | async-start | bytes 4194304 | tf_op jit(solution)/shard_map/all_to_all | solution.py:176
  129.8 5.9 %collective-permute-start.9 = (bf16[256,1792]{1,0:T(8,128)(2,1)}, bf16[256,1792]{1,0:T(8,128)(2,1)S(1)}, u32[]{:S(2)}, u32[]{:S(2)}) collective-permute-start(bf16[256,1792]{1,0:T(8,128)(2,1)} %get-tuple-element.53), channel_id=1, source_target_pairs={{0,8},{8,0},{1,9},{9,1},{2,10},{10,2},{3,11},{11,3},{4,12},{12,4},... | collective-permute-start | bytes 2752520 | tf_op jit(solution)/shard_map/ppermute | solution.py:23
  135.7 0.9 copy-start.3
  145.7 35.6 %copy-start.1 = (f32[256,1792]{1,0:T(8,128)S(1)}, f32[256,1792]{1,0:T(8,128)}, u32[]{:S(2)}) copy-start(f32[256,1792]{1,0:T(8,128)} %get-tuple-element.57) | copy-start | bytes 5505028
  145.7 10.8 %all-to-all-start.4 = ((f32[16,1,128]{2,1,0:T(1,128)}), f32[16,1,128]{2,1,0:T(1,128)S(1)}, u32[]{:S(2)}, u32[]{:S(2)}) async-start(f32[16,1,128]{2,1,0:T(1,128)} %bitcast.33), calls=%async_computation.4 | async-start | bytes 16384 | tf_op jit(solution)/shard_map/all_to_all | solution.py:208
Sparse Core Ops, SparseCore 0:
  10.4 88.8 all-gather.1

commit v3 on v2

--- a/solution.py
+++ b/solution.py
@@ -1,3 +1,5 @@
+import functools
+
 import jax
 import jax.numpy as jnp
 from jax import lax
@@ -65,14 +67,15 @@
     return copies
 
 
-def part_kernel(*refs):
-    pieces, (weight_ref, part_ref, tokens_ref, sems) = refs[:6], refs[6:]
-    copies = fetch(pieces, tokens_ref, sems)
-    for half in range(2):
-        for copy in copies[1:] if half else copies[:1]:
-            copy.wait()
-        part = dot(tokens_ref[1024 * half : 1024 * half + 1024], weight_ref[...], 1, 1)
-        part_ref[:, 16 * half : 16 * half + 16] = part.reshape(16, 8, 8, 512).swapaxes(0, 1).astype(BF)
+def part_kernel(count, at, *refs):
+    pieces, weight_ref, (part_ref, tokens_ref, staged_ref, sems, out_sem) = refs[:count], refs[count], refs[-5:]
+    for copy in fetch(pieces, tokens_ref, sems):
+        copy.wait()
+    part = dot(tokens_ref[...], weight_ref[...], 1, 1)
+    staged_ref[...] = part.reshape(16, 8, 8, 512).swapaxes(0, 1).astype(BF)
+    copy = pltpu.make_async_copy(staged_ref, part_ref.at[:, pl.ds(at, 16)], out_sem)
+    copy.start()
+    copy.wait()
 
 
 def grad_kernel(*refs):
@@ -151,36 +154,46 @@
     rows = jnp.stack([rows[1].swapaxes(0, 1), rolled(rolled(rows[0], 0, y), 1, zh)])
     copies = jnp.broadcast_to(rows.reshape(1, 2, 16, 8, 512), (8, 2, 16, 8, 512))
     feats = lax.all_to_all(copies, TP, split_axis=0, concat_axis=0, tiled=True)
-    *y2, second = sync(*middle(y1, y3, "y"), second)
+    y2 = middle(y1, y3, "y")
 
     weight = master_late.astype(BF)
     weight_other = shift(weight, "c", 1, 2)
     both = jnp.where(c == 0, cat(weight, weight_other), cat(weight_other, weight))
     both, second = sync(both, second)
 
-    *y2, both, y0, y1, y3, second = sync(*y2, both, y0, y1, y3, second)
-
-    vmem, anywhere = (pl.BlockSpec(memory_space=space) for space in (pltpu.VMEM, pltpu.HBM))
+    vmem, hbm = (pl.BlockSpec(memory_space=space) for space in (pltpu.VMEM, pltpu.HBM))
+    limit = pltpu.CompilerParams(vmem_limit_bytes=60 << 20)
+
+    def partials(pieces, at, *buffer):
+        count = len(pieces)
+        return pl.pallas_call(
+            functools.partial(part_kernel, count, at),
+            in_specs=[hbm] * count + [vmem] + [hbm] * len(buffer),
+            out_specs=hbm,
+            out_shape=jax.ShapeDtypeStruct((8, 32, 8, 512), BF),
+            input_output_aliases={count + 1: 0} if buffer else {},
+            scratch_shapes=[
+                pltpu.VMEM((1024, 1792), BF),
+                pltpu.VMEM((8, 16, 8, 512), BF),
+                pltpu.SemaphoreType.DMA((count,)),
+                pltpu.SemaphoreType.DMA,
+            ],
+            compiler_params=limit,
+            cost_estimate=cost(2 * 1024 * 512 * 1792, 8 << 20),
+        )(*pieces, both, *buffer)
+
+    part = partials([second], 0)
+    *y2, y0, y1, y3, second, part = sync(*y2, y0, y1, y3, second, part)
+    part = partials([y0, y1, *y2, y3], 16, part)
     pieces = (second, y0, y1, *y2, y3)
-    scratch = [pltpu.VMEM((2048, 1792), BF), pltpu.SemaphoreType.DMA((6,))]
-    limit = pltpu.CompilerParams(vmem_limit_bytes=60 << 20)
-    part = pl.pallas_call(
-        part_kernel,
-        in_specs=[anywhere] * 6 + [vmem],
-        out_specs=vmem,
-        out_shape=jax.ShapeDtypeStruct((8, 32, 8, 512), BF),
-        scratch_shapes=scratch,
-        compiler_params=limit,
-        cost_estimate=cost(2 * 2048 * 512 * 1792, 12 << 20),
-    )(*pieces, both)
     got = lax.all_to_all(part, TP, split_axis=0, concat_axis=0, tiled=True)
     feats, _ = sync(feats, part)
     grad, grad_other = pl.pallas_call(
         grad_kernel,
-        in_specs=[anywhere] * 6 + [vmem],
+        in_specs=[hbm] * 6 + [vmem],
         out_specs=[vmem] * 2,
         out_shape=[f32, jax.ShapeDtypeStruct((256, 1792), BF)],
-        scratch_shapes=scratch,
+        scratch_shapes=[pltpu.VMEM((2048, 1792), BF), pltpu.SemaphoreType.DMA((6,))],
         compiler_params=limit,
         cost_estimate=cost(2 * 2048 * 512 * 1792, 12 << 20),
     )(*pieces, feats)

time: 190 us -> 190 us (level)
  waiting for transfers between devices: 61.1 us -> 56.1 us
  Pallas kernels: 26.3 us -> 30.4 us
    ppermute x10, waiting for transfers between devices: 52.1 us -> 37.2 us  [shift(): lax.ppermute(value, axis, [(i, (i - by) % size) for i in range(size)])]
    all_gather x1, waiting for transfers between devices: 0.01 us -> 6.4 us  [on_device(): lax.all_gather(halves[:, 1].reshape(64, 1792), CH, axis=0, tiled=True)]
    pallas_call x2 -> x3, Pallas kernels: 19.4 us -> 23.5 us  [the longest x2 13.3 us: partials(): pl.pallas_call(functools.partial(part_kernel, count, at), in_specs=[hbm]...]
    all_to_all x1, waiting for transfers between devices: 2.19 us -> 5.11 us  [on_device(): got = lax.all_to_all(part, TP, split_axis=0, concat_axis=0, tiled=True)]
  transfers between devices with their start and end apart: 16 -> 16, of which waited for: 11 -> 11; matrix products, arithmetic and copies ran while one was open for 3% -> 3% of each run, Pallas kernels for 13% -> 16%
where the time goes in v3:
time: 190 us; the launch traced here: 189 us
  waiting for transfers between devices  56.1 us (30%)
  starting transfers between devices  52.7 us (28%)
  Pallas kernels  30.4 us (16%)
  blocking collectives  21.2 us (11%)
  between operations  15.8 us (8%)
  local copies, waits for them, and re-layouts  9.36 us (5%)
  other arithmetic  3.9 us (2%)
    ppermute x10, waiting for transfers between devices, shift(): lax.ppermute(value, axis, [(i, (i - by) % size) for i in range(size)])  37.2 us
    all_to_all x1, blocking collectives, on_device(): out = lax.all_to_all(out, CH, split_axis=0, concat_axis=0, tiled=True)  21.2 us
    ppermute x10, starting transfers between devices, shift(): lax.ppermute(value, axis, [(i, (i - by) % size) for i in range(size)])  20.8 us
    pallas_call x2, Pallas kernels, partials(): pl.pallas_call(functools.partial(part_kernel, count, at), in_specs=[hbm]...  13.3 us
    all_to_all x1, starting transfers between devices, on_device(): feats = lax.all_to_all(copies, TP, split_axis=0, concat_axis=0, tiled=True)  11.6 us
    pallas_call x1, Pallas kernels, on_device(): pl.pallas_call(grad_kernel, in_specs=[hbm] * 6 + [vmem], out_specs=[vmem]...  10.2 us
    all_gather x1, waiting for transfers between devices, on_device(): lax.all_gather(halves[:, 1].reshape(64, 1792), CH, axis=0, tiled=True)  6.4 us
    all_to_all x1, starting transfers between devices, on_device(): lax.all_to_all(activations, TP, split_axis=0, concat_axis=1, tiled=True)  6.22 us
  transfers between devices with their start and end apart: 16, of which 11 were waited for; matrix products, arithmetic and copies ran while one was open for 3% of the time, Pallas kernels for 16%

profile of v3, /device:TPU:1, one launch (start us, length us, event | category | flops | bytes accessed | tf_op | source)
XLA Modules:
  0.0 189.5 jit_solution(8768574403753664070)
XLA Ops:
  7.2 0.0 all-gather.2.cloned.1.call-start
  7.2 1.8 slice_bitcast_fusion.1
  9.0 0.0 all-gather.2.cloned.1.call-update
  9.0 6.2 %all-to-all-start = ((bf16[8,16,1024]{2,1,0:T(8,128)(2,1)}), bf16[8,16,1024]{2,1,0:T(8,128)(2,1)S(1)}, u32[]{:S(2)}, u32[]{:S(2)}) async-start(bf16[8,16,1024]{2,1,0:T(8,128)(2,1)} %bitcast.68), calls=%async_computation | async-start | bytes 524288 | tf_op jit(solution)/shard_map/all_to_all | solution.py:144
  15.2 5.1 %collective-permute-start = (bf16[64,1792]{1,0:T(8,128)(2,1)S(1)}, bf16[64,1792]{1,0:T(8,128)(2,1)S(1)}, u32[]{:S(2)}, u32[]{:S(2)}) collective-permute-start(bf16[64,1792]{1,0:T(8,128)(2,1)S(1)} %get-tuple-element.55), channel_id=1, source_target_pairs={{0,192},{64,0},{128,64},{192,128},{1,193},{65,1},{129,65},{193,129... | collective-permute-start | bytes 688136 | tf_op jit(solution)/shard_map/ppermute | solution.py:25
  20.4 0.0 collective-permute-start.1
  20.4 1.0 all-to-all-done
  21.4 3.1 %collective-permute-done = bf16[64,1792]{1,0:T(8,128)(2,1)S(1)} collective-permute-done((bf16[64,1792]{1,0:T(8,128)(2,1)S(1)}, bf16[64,1792]{1,0:T(8,128)(2,1)S(1)}, u32[]{:S(2)}, u32[]{:S(2)}) %collective-permute-start) | collective-permute-done | bytes 229408 | tf_op jit(solution)/shard_map/ppermute | solution.py:25
  24.5 5.0 %collective-permute-done.1 = bf16[64,1792]{1,0:T(8,128)(2,1)S(1)} collective-permute-done((bf16[64,1792]{1,0:T(8,128)(2,1)S(1)}, bf16[64,1792]{1,0:T(8,128)(2,1)S(1)}, u32[]{:S(2)}, u32[]{:S(2)}) %collective-permute-start.1) | collective-permute-done | bytes 229408 | tf_op jit(solution)/shard_map/ppermute | solution.py:25
  29.5 0.7 copy.37
  30.2 5.6 %all-to-all-start.1 = ((bf16[16,16,512]{2,0,1:T(8,128)(2,1)}), bf16[16,16,512]{2,0,1:T(8,128)(2,1)S(1)}, u32[]{:S(2)}, u32[]{:S(2)}) async-start(bf16[16,16,512]{2,0,1:T(8,128)(2,1)} %bitcast.58), calls=%async_computation.1 | async-start | bytes 524288 | tf_op jit(solution)/shard_map/all_to_all | solution.py:147
  35.9 3.6 %collective-permute-start.2 = (bf16[32,1792]{1,0:T(8,128)(2,1)S(1)}, bf16[32,1792]{1,0:T(8,128)(2,1)S(1)}, u32[]{:S(2)}, u32[]{:S(2)}) collective-permute-start(bf16[32,1792]{1,0:T(8,128)(2,1)S(1)} %slice.43), channel_id=1, source_target_pairs={{0,192},{64,0},{128,64},{192,128},{1,193},{65,1},{129,65},{193,129... | collective-permute-start | bytes 344072 | tf_op jit(solution)/shard_map/ppermute | solution.py:25
  39.4 0.1 collective-permute-start.3
  39.5 4.2 %collective-permute-done.2 = bf16[32,1792]{1,0:T(8,128)(2,1)S(1)} collective-permute-done((bf16[32,1792]{1,0:T(8,128)(2,1)S(1)}, bf16[32,1792]{1,0:T(8,128)(2,1)S(1)}, u32[]{:S(2)}, u32[]{:S(2)}) %collective-permute-start.2) | collective-permute-done | bytes 114720 | tf_op jit(solution)/shard_map/ppermute | solution.py:25
  43.7 2.7 %collective-permute-done.3 = bf16[32,1792]{1,0:T(8,128)(2,1)S(1)} collective-permute-done((bf16[32,1792]{1,0:T(8,128)(2,1)S(1)}, bf16[32,1792]{1,0:T(8,128)(2,1)S(1)}, u32[]{:S(2)}, u32[]{:S(2)}) %collective-permute-start.3) | collective-permute-done | bytes 114720 | tf_op jit(solution)/shard_map/ppermute | solution.py:25
  46.4 1.0 all-to-all-done.1
  47.4 0.1 fusion
  47.6 0.1 fusion.2
  47.7 0.1 fusion.1
  47.8 1.5 broadcast_in_dim.11
  49.3 11.6 %all-to-all-start.2 = ((bf16[8,2,16,8,512]{4,3,2,1,0:T(8,128)(2,1)}), bf16[8,2,16,8,512]{4,3,2,1,0:T(8,128)(2,1)}, u32[]{:S(2)}, u32[]{:S(2)}) async-start(bf16[8,2,16,8,512]{4,3,2,1,0:T(8,128)(2,1)} %broadcast_in_dim.11), calls=%async_computation.2 | async-start | bytes 4194304 | tf_op jit(solution)/shard_map/all_to_all | solution.py:156
  60.9 0.0 copy-done.5
  61.0 0.0 copy-start.4
  61.0 2.2 %collective-permute-start.4 = (bf16[256,1792]{1,0:T(8,128)(2,1)S(1)}, bf16[256,1792]{1,0:T(8,128)(2,1)S(1)}, u32[]{:S(2)}, u32[]{:S(2)}) collective-permute-start(bf16[256,1792]{1,0:T(8,128)(2,1)S(1)} %constant_dynamic-update-slice_fusion.refs_0_.refs_1_), channel_id=1, source_target_pairs={{0,48},{16,0},{32,16},{48,32},{1,49},{17,1},{33,17},{49,33},{2,50}... | collective-permute-start | bytes 2752520 | tf_op jit(solution)/shard_map/ppermute | solution.py:25
  63.2 0.0 collective-permute-start.6
  63.2 0.0 copy-done
  63.2 0.1 convert_element_type.14
  63.3 4.8 %collective-permute-start.8 = (bf16[256,1792]{1,0:T(8,128)(2,1)S(1)}, bf16[256,1792]{1,0:T(8,128)(2,1)S(1)}, u32[]{:S(2)}, u32[]{:S(2)}) collective-permute-start(bf16[256,1792]{1,0:T(8,128)(2,1)S(1)} %convert_element_type.14), channel_id=1, source_target_pairs={{0,8},{8,0},{1,9},{9,1},{2,10},{10,2},{3,11},{11,3},{4,12},{12,4},... | collective-permute-start | bytes 2752520 | tf_op jit(solution)/shard_map/ppermute | solution.py:25
  68.0 20.0 %collective-permute-done.4.refs_1_.refs_2_ = bf16[256,1792]{1,0:T(8,128)(2,1)S(1)} collective-permute-done((bf16[256,1792]{1,0:T(8,128)(2,1)S(1)}, bf16[256,1792]{1,0:T(8,128)(2,1)S(1)}, u32[]{:S(2)}, u32[]{:S(2)}) %collective-permute-start.4) | collective-permute-done | bytes 917536 | tf_op jit(solution)/shard_map/ppermute | solution.py:25
  88.0 0.9 copy-done.1
  89.0 0.0 copy-done.4
  89.0 3.6 %collective-permute-start.5 = (bf16[128,1792]{1,0:T(8,128)(2,1)S(1)}, bf16[128,1792]{1,0:T(8,128)(2,1)S(1)}, u32[]{:S(2)}, u32[]{:S(2)}) collective-permute-start(bf16[128,1792]{1,0:T(8,128)(2,1)S(1)} %slice.57), channel_id=1, source_target_pairs={{0,48},{16,0},{32,16},{48,32},{1,49},{17,1},{33,17},{49,33},{2,50}... | collective-permute-start | bytes 1376264 | tf_op jit(solution)/shard_map/ppermute | solution.py:25
  92.6 0.0 collective-permute-done.6.refs_4_.refs_5_
  92.6 0.9 copy-done.2
  93.5 0.1 collective-permute-start.7
  93.6 0.0 collective-permute-done.8
  93.6 2.0 %maximum_select_fusion.refs_1_.refs_5_ = bf16[512,1792]{1,0:T(8,128)(2,1)} fusion(bf16[256,1792]{1,0:T(8,128)(2,1)S(1)} %collective-permute-done.8, bf16[256,1792]{1,0:T(8,128)(2,1)S(1)} %convert_element_type.14, pred[]{:T(512)S(6)} %eq.36), kind=kLoop, calls=%fused_computation | loop fusion | flops 8257536 | bytes 3670017 | tf_op jit(solution)/shard_map/jit(_where)/select_n | solution.py:161
  95.6 6.4 %all-gather.2.cloned.1.call-done.refs_0_ = bf16[1024,1792]{1,0:T(8,128)(2,1)} async-done(((bf16[64,1792]{1,0:T(8,128)(2,1)}), bf16[1024,1792]{1,0:T(8,128)(2,1)}) %all-gather.2.cloned.1.call-update) | async-done | bytes 3670032 | tf_op jit(solution)/shard_map/all_gather | solution.py:140
  102.0 6.7 %shard_map.84.refs_6_ = bf16[8,32,8,512]{3,2,1,0:T(8,128)(2,1)} custom-call(bf16[1024,1792]{1,0:T(8,128)(2,1)} %all-gather.2.cloned.1.call-done.refs_0_, bf16[512,1792]{1,0:T(8,128)(2,1)} %maximum_select_fusion.refs_1_.refs_5_), custom_call_target="tpu_custom_call" | custom-call | flops 1879048192 | bytes 8388608 | tf_op jit(solution)/shard_map/pallas_call | solution.py:169
  108.7 0.0 collective-permute-done.5.refs_2_.refs_3_
  108.7 0.0 copy-start.7
  108.7 0.0 collective-permute-done.7.refs_3_.refs_4_
  108.7 0.8 copy-done.7
  109.5 6.7 %shard_map.85 = bf16[8,32,8,512]{3,2,1,0:T(8,128)(2,1)} custom-call(bf16[256,1792]{1,0:T(8,128)(2,1)} %copy-done.4, bf16[256,1792]{1,0:T(8,128)(2,1)} %copy-done.1, bf16[128,1792]{1,0:T(8,128)(2,1)} %copy-done.7, bf16[128,1792]{1,0:T(8,128)(2,1)} %collective-permute-done.7.refs_3_.refs_4_, ...), custom_call_target="tpu_custom_call", output_to_operand_aliasing={{}: (6, {})} | custom-call | flops 1879048192 | bytes 8388608 | tf_op jit(solution)/shard_map/pallas_call | solution.py:169
  116.1 0.0 all-to-all-done.2.refs_6_
  116.1 3.8 %all-to-all-start.3 = ((bf16[8,32,8,512]{3,2,1,0:T(8,128)(2,1)}), bf16[8,32,8,512]{3,2,1,0:T(8,128)(2,1)S(1)}, u32[]{:S(2)}, u32[]{:S(2)}) async-start(bf16[8,32,8,512]{3,2,1,0:T(8,128)(2,1)} %shard_map.85), calls=%async_computation.3 | async-start | bytes 4194304 | tf_op jit(solution)/shard_map/all_to_all | solution.py:189
  120.0 10.2 %shard_map.86 = (f32[256,1792]{1,0:T(8,128)}, bf16[256,1792]{1,0:T(8,128)(2,1)}) custom-call(bf16[1024,1792]{1,0:T(8,128)(2,1)} %all-gather.2.cloned.1.call-done.refs_0_, bf16[256,1792]{1,0:T(8,128)(2,1)} %copy-done.4, bf16[256,1792]{1,0:T(8,128)(2,1)} %copy-done.1, bf16[128,1792]{1,0:T(8,128)(2,1)} %copy-done.7, ...), custom_call_target="tpu_custom_call" | custom-call | flops 3758096384 | bytes 12582912 | tf_op jit(solution)/shard_map/pallas_call | solution.py:191
  130.2 1.5 collective-permute-start.9
  131.7 0.1 stack.79.places_ref
  131.8 2.2 %collective-permute-done.9.other_ref = bf16[256,1792]{1,0:T(8,128)(2,1)S(1)} collective-permute-done((bf16[256,1792]{1,0:T(8,128)(2,1)}, bf16[256,1792]{1,0:T(8,128)(2,1)S(1)}, u32[]{:S(2)}, u32[]{:S(2)}) %collective-permute-start.9) | collective-permute-done | bytes 917536 | tf_op jit(solution)/shard_map/ppermute | solution.py:25
  134.0 0.9 copy-done.6
  134.9 6.1 %shard_map.87 = (f32[256,1792]{1,0:T(8,128)}, f32[256,1792]{1,0:T(8,128)}, f32[256,1792]{1,0:T(8,128)}, f32[16,128]{1,0:T(8,128)}) custom-call(f32[256,1792]{1,0:T(8,128)} %get-tuple-element.46.grad_ref, bf16[256,1792]{1,0:T(8,128)(2,1)} %copy-done.6, f32[256,1792]{1,0:T(8,128)} %one_ref.1, f32[256,1792]{1,0:T(8,128)} %two_ref.1, f32[256,1792]{1,0:T(8,128)} %master_ref.1), custom_call_target="tpu_custom_call" | custom-call | bytes 8388608 | tf_op jit(solution)/shard_map/pallas_call | solution.py:210
  141.0 5.1 %all-to-all-done.3.got_ref = bf16[8,32,8,512]{3,2,1,0:T(8,128)(2,1)S(1)} async-done(((bf16[8,32,8,512]{3,2,1,0:T(8,128)(2,1)}), bf16[8,32,8,512]{3,2,1,0:T(8,128)(2,1)S(1)}, u32[]{:S(2)}, u32[]{:S(2)}) %all-to-all-start.3) | async-done | bytes 2097184 | tf_op jit(solution)/shard_map/all_to_all | solution.py:189
  146.1 0.8 shard_map.88
  146.9 0.0 copy-start.3
  146.9 4.6 %all-to-all-start.4 = ((f32[16,1,128]{2,1,0:T(1,128)}), f32[16,1,128]{2,1,0:T(1,128)S(1)}, u32[]{:S(2)}, u32[]{:S(2)}) async-start(f32[16,1,128]{2,1,0:T(1,128)} %bitcast.33), calls=%async_computation.4 | async-start | bytes 16384 | tf_op jit(solution)/shard_map/all_to_all | solution.py:221
  151.6 5.4 %all-to-all-done.4 = f32[16,1,128]{2,1,0:T(1,128)S(1)} async-done(((f32[16,1,128]{2,1,0:T(1,128)}), f32[16,1,128]{2,1,0:T(1,128)S(1)}, u32[]{:S(2)}, u32[]{:S(2)}) %all-to-all-start.4) | async-done | bytes 8224 | tf_op jit(solution)/shard_map/all_to_all | solution.py:221
  157.0 0.1 fusion.8
  157.2 21.2 %all_to_all.62 = bf16[16,24,512]{2,1,0:T(8,128)(2,1)S(1)} all-to-all(bf16[16,24,512]{2,1,0:T(8,128)(2,1)S(1)} %pad_maximum_fusion), channel_id=1, replica_groups=mesh['zh'=4,'y'=4,'c'=2,'zl'=2,'x'=4] {'zh','y'}, dimensions={0} | all-to-all | bytes 786432 | tf_op jit(solution)/shard_map/all_to_all | solution.py:225
  178.4 0.1 reduce_sum.27
  178.5 0.6 fusion.12
  180.5 0.7 copy.35
  181.3 0.0 copy-done.3
  181.3 1.4 broadcast_multiply_fusion
  (27 shorter events, 0.4 us)
Async XLA Ops:
  7.2 94.8 %all-gather.2.cloned.1.call-start = ((), (), s32[]{:S(2)}) async-start(), calls=%async_computation.6 | async-start | bytes 3899392 | tf_op jit(solution)/shard_map/all_gather | solution.py:140
  9.0 12.3 %all-to-all-start = ((bf16[8,16,1024]{2,1,0:T(8,128)(2,1)}), bf16[8,16,1024]{2,1,0:T(8,128)(2,1)S(1)}, u32[]{:S(2)}, u32[]{:S(2)}) async-start(bf16[8,16,1024]{2,1,0:T(8,128)(2,1)} %bitcast.68), calls=%async_computation | async-start | bytes 524288 | tf_op jit(solution)/shard_map/all_to_all | solution.py:144
  15.2 9.2 %collective-permute-start = (bf16[64,1792]{1,0:T(8,128)(2,1)S(1)}, bf16[64,1792]{1,0:T(8,128)(2,1)S(1)}, u32[]{:S(2)}, u32[]{:S(2)}) collective-permute-start(bf16[64,1792]{1,0:T(8,128)(2,1)S(1)} %get-tuple-element.55), channel_id=1, source_target_pairs={{0,192},{64,0},{128,64},{192,128},{1,193},{65,1},{129,65},{193,129... | collective-permute-start | bytes 688136 | tf_op jit(solution)/shard_map/ppermute | solution.py:25
  20.4 9.1 %collective-permute-start.1 = (bf16[64,1792]{1,0:T(8,128)(2,1)S(1)}, bf16[64,1792]{1,0:T(8,128)(2,1)S(1)}, u32[]{:S(2)}, u32[]{:S(2)}) collective-permute-start(bf16[64,1792]{1,0:T(8,128)(2,1)S(1)} %get-tuple-element.55), channel_id=1, source_target_pairs={{0,64},{64,128},{128,192},{192,0},{1,65},{65,129},{129,193},{193,1... | collective-permute-start | bytes 688136 | tf_op jit(solution)/shard_map/ppermute | solution.py:25
  30.2 17.2 %all-to-all-start.1 = ((bf16[16,16,512]{2,0,1:T(8,128)(2,1)}), bf16[16,16,512]{2,0,1:T(8,128)(2,1)S(1)}, u32[]{:S(2)}, u32[]{:S(2)}) async-start(bf16[16,16,512]{2,0,1:T(8,128)(2,1)} %bitcast.58), calls=%async_computation.1 | async-start | bytes 524288 | tf_op jit(solution)/shard_map/all_to_all | solution.py:147
  35.9 7.8 %collective-permute-start.2 = (bf16[32,1792]{1,0:T(8,128)(2,1)S(1)}, bf16[32,1792]{1,0:T(8,128)(2,1)S(1)}, u32[]{:S(2)}, u32[]{:S(2)}) collective-permute-start(bf16[32,1792]{1,0:T(8,128)(2,1)S(1)} %slice.43), channel_id=1, source_target_pairs={{0,192},{64,0},{128,64},{192,128},{1,193},{65,1},{129,65},{193,129... | collective-permute-start | bytes 344072 | tf_op jit(solution)/shard_map/ppermute | solution.py:25
  39.4 7.0 %collective-permute-start.3 = (bf16[32,1792]{1,0:T(8,128)(2,1)S(1)}, bf16[32,1792]{1,0:T(8,128)(2,1)S(1)}, u32[]{:S(2)}, u32[]{:S(2)}) collective-permute-start(bf16[32,1792]{1,0:T(8,128)(2,1)S(1)} %slice.44), channel_id=1, source_target_pairs={{0,64},{64,128},{128,192},{192,0},{1,65},{65,129},{129,193},{193,1... | collective-permute-start | bytes 344072 | tf_op jit(solution)/shard_map/ppermute | solution.py:25
  49.3 11.6 %copy-start.5 = (bf16[128,1792]{1,0:T(8,128)(2,1)S(1)}, bf16[128,1792]{1,0:T(8,128)(2,1)}, u32[]{:S(2)}) copy-start(bf16[128,1792]{1,0:T(8,128)(2,1)} %param.6) | copy-start | bytes 1376260
  49.3 13.9 %copy-start = (f32[256,1792]{1,0:T(8,128)S(1)}, f32[256,1792]{1,0:T(8,128)}, u32[]{:S(2)}) copy-start(f32[256,1792]{1,0:T(8,128)} %master_ref.1) | copy-start | bytes 5505028
  49.3 66.8 %all-to-all-start.2 = ((bf16[8,2,16,8,512]{4,3,2,1,0:T(8,128)(2,1)}), bf16[8,2,16,8,512]{4,3,2,1,0:T(8,128)(2,1)}, u32[]{:S(2)}, u32[]{:S(2)}) async-start(bf16[8,2,16,8,512]{4,3,2,1,0:T(8,128)(2,1)} %broadcast_in_dim.11), calls=%async_computation.2 | async-start | bytes 4194304 | tf_op jit(solution)/shard_map/all_to_all | solution.py:156
  61.0 28.0 %copy-start.4 = (bf16[256,1792]{1,0:T(8,128)(2,1)}, bf16[256,1792]{1,0:T(8,128)(2,1)S(1)}, u32[]{:S(2)}) copy-start(bf16[256,1792]{1,0:T(8,128)(2,1)S(1)} %constant_dynamic-update-slice_fusion.refs_0_.refs_1_) | copy-start | bytes 2752516
  61.0 27.0 %collective-permute-start.4 = (bf16[256,1792]{1,0:T(8,128)(2,1)S(1)}, bf16[256,1792]{1,0:T(8,128)(2,1)S(1)}, u32[]{:S(2)}, u32[]{:S(2)}) collective-permute-start(bf16[256,1792]{1,0:T(8,128)(2,1)S(1)} %constant_dynamic-update-slice_fusion.refs_0_.refs_1_), channel_id=1, source_target_pairs={{0,48},{16,0},{32,16},{48,32},{1,49},{17,1},{33,17},{49,33},{2,50}... | collective-permute-start | bytes 2752520 | tf_op jit(solution)/shard_map/ppermute | solution.py:25
  63.2 29.4 %collective-permute-start.6 = (bf16[256,1792]{1,0:T(8,128)(2,1)S(1)}, bf16[256,1792]{1,0:T(8,128)(2,1)S(1)}, u32[]{:S(2)}, u32[]{:S(2)}) collective-permute-start(bf16[256,1792]{1,0:T(8,128)(2,1)S(1)} %constant_dynamic-update-slice_fusion.refs_0_.refs_1_), channel_id=1, source_target_pairs={{0,16},{16,32},{32,48},{48,0},{1,17},{17,33},{33,49},{49,1},{2,18}... | collective-permute-start | bytes 2752520 | tf_op jit(solution)/shard_map/ppermute | solution.py:25
  63.3 30.3 %collective-permute-start.8 = (bf16[256,1792]{1,0:T(8,128)(2,1)S(1)}, bf16[256,1792]{1,0:T(8,128)(2,1)S(1)}, u32[]{:S(2)}, u32[]{:S(2)}) collective-permute-start(bf16[256,1792]{1,0:T(8,128)(2,1)S(1)} %convert_element_type.14), channel_id=1, source_target_pairs={{0,8},{8,0},{1,9},{9,1},{2,10},{10,2},{3,11},{11,3},{4,12},{12,4},... | collective-permute-start | bytes 2752520 | tf_op jit(solution)/shard_map/ppermute | solution.py:25
  88.0 0.9 copy-start.1
  89.0 19.7 %collective-permute-start.5 = (bf16[128,1792]{1,0:T(8,128)(2,1)S(1)}, bf16[128,1792]{1,0:T(8,128)(2,1)S(1)}, u32[]{:S(2)}, u32[]{:S(2)}) collective-permute-start(bf16[128,1792]{1,0:T(8,128)(2,1)S(1)} %slice.57), channel_id=1, source_target_pairs={{0,48},{16,0},{32,16},{48,32},{1,49},{17,1},{33,17},{49,33},{2,50}... | collective-permute-start | bytes 1376264 | tf_op jit(solution)/shard_map/ppermute | solution.py:25
  92.6 0.9 copy-start.2
  93.5 15.2 %collective-permute-start.7 = (bf16[128,1792]{1,0:T(8,128)(2,1)S(1)}, bf16[128,1792]{1,0:T(8,128)(2,1)}, u32[]{:S(2)}, u32[]{:S(2)}) collective-permute-start(bf16[128,1792]{1,0:T(8,128)(2,1)S(1)} %slice.58), channel_id=1, source_target_pairs={{0,16},{16,32},{32,48},{48,0},{1,17},{17,33},{33,49},{49,1},{2,18}... | collective-permute-start | bytes 1376264 | tf_op jit(solution)/shard_map/ppermute | solution.py:25
  108.7 0.8 copy-start.7
  116.1 30.0 %all-to-all-start.3 = ((bf16[8,32,8,512]{3,2,1,0:T(8,128)(2,1)}), bf16[8,32,8,512]{3,2,1,0:T(8,128)(2,1)S(1)}, u32[]{:S(2)}, u32[]{:S(2)}) async-start(bf16[8,32,8,512]{3,2,1,0:T(8,128)(2,1)} %shard_map.85), calls=%async_computation.3 | async-start | bytes 4194304 | tf_op jit(solution)/shard_map/all_to_all | solution.py:189
  130.2 3.8 %collective-permute-start.9 = (bf16[256,1792]{1,0:T(8,128)(2,1)}, bf16[256,1792]{1,0:T(8,128)(2,1)S(1)}, u32[]{:S(2)}, u32[]{:S(2)}) collective-permute-start(bf16[256,1792]{1,0:T(8,128)(2,1)} %get-tuple-element.47), channel_id=1, source_target_pairs={{0,8},{8,0},{1,9},{9,1},{2,10},{10,2},{3,11},{11,3},{4,12},{12,4},... | collective-permute-start | bytes 2752520 | tf_op jit(solution)/shard_map/ppermute | solution.py:25
  134.0 0.9 copy-start.6
  146.9 34.3 %copy-start.3 = (f32[256,1792]{1,0:T(8,128)S(1)}, f32[256,1792]{1,0:T(8,128)}, u32[]{:S(2)}) copy-start(f32[256,1792]{1,0:T(8,128)} %get-tuple-element.51) | copy-start | bytes 5505028
  146.9 10.1 %all-to-all-start.4 = ((f32[16,1,128]{2,1,0:T(1,128)}), f32[16,1,128]{2,1,0:T(1,128)S(1)}, u32[]{:S(2)}, u32[]{:S(2)}) async-start(f32[16,1,128]{2,1,0:T(1,128)} %bitcast.33), calls=%async_computation.4 | async-start | bytes 16384 | tf_op jit(solution)/shard_map/all_to_all | solution.py:221
Sparse Core Ops, SparseCore 0:
  10.4 91.5 all-gather.1
